TPU v7x, 256 devices: a whole 4x4x8 slice. The times are simulated.
256 devices in a mesh: emb: 64 (over x, z, core), sec: 4 (over y).
Axes of the slice: x: 4, y: 4, z: 8, core: 2. Of those that a mesh axis runs over, the one named last changes fastest.
Arguments:
- emb_table: float32 [32, 32768, 64], P('sec', 'emb'), may hold values from -4 to 4
- emb_accum: float32 [32, 32768, 64], P('sec', 'emb'), may hold values from 1e-05 to 0.001
- slot_ids: int32 [16384, 32, 2], P('emb', 'sec'), may hold values from 0 to 32767, as said below
- bag_len: int32 [16384, 32], P('emb', 'sec'), may hold values from 1 to 2
- expert_w: bfloat16 [2048, 2048], P(None, 'sec'), may hold values from -0.125 to 0.125
- tower_w: bfloat16 [2048, 2048], P(None, 'sec'), may hold values from -0.125 to 0.125
- tower_out: float32 [4, 512], P('sec'), may hold values from -0.25 to 0.25
- section_task: int32 [4], P('sec'), may hold values from 0 to 2, as said below
- click_like: float32 [16384, 2], P('emb'), may hold values from 0 to 1
- watch: float32 [16384], P('emb'), may hold values from -3 to 3
Outputs:
- new_table: float32 [32, 32768, 64], P('sec', 'emb')
- new_accum: float32 [32, 32768, 64], P('sec', 'emb')
- expert_grad: float32 [2048, 2048], P('emb', 'sec')
- tower_grad: float32 [2048, 2048], P('emb', 'sec')
- head_grad: float32 [4, 512], P('sec')
Inputs may be any that keep to these rules, and one draw needn't show every extreme that they name: `slot_ids`: the shard of id r is r // 512. Of the 4096 ids of one device (the examples of one emb index, the slots of one sec index), at most 128 fall in one shard, bag positions beyond bag_len included; in every draw one shard gets exactly 128 from every device. `section_task`: each of the 3 tasks owns at least one section.
All inputs are finite; a program needn't handle non-finite values.
Results may differ from a plain program's by a relative error of at most 0.017.
Values may be sent and summed in bfloat16 or wider, within the bound.
A program may use at most 128 MiB of HBM per device.

v0:
```python
import jax
import jax.numpy as jnp
from jax import lax
from jax.sharding import PartitionSpec as P

learn_rate = 0.2


def silu_slope(value):
    logistic = jax.nn.sigmoid(value)
    return logistic * (1.0 + value * (1.0 - logistic))


def body(
    emb_table,
    emb_accum,
    slot_ids,
    bag_len,
    expert_w,
    tower_w,
    tower_out,
    section_task,
    click_like,
    watch,
):
    groups = lax.axis_size("emb")
    slots_here, table_rows, row_width = emb_table.shape
    examples_here, _, bag_size = slot_ids.shape
    count = examples_here * slots_here * bag_size
    capacity = 2 * count // groups
    owners = (slot_ids // table_rows).reshape(-1)
    slot_local = lax.broadcasted_iota(jnp.int32, slot_ids.shape, 1)
    row_keys = (slot_local * table_rows + slot_ids % table_rows).reshape(-1)
    sort_order = jnp.argsort(owners, stable=True)
    sorted_owner = owners[sort_order]
    shard_ids = jnp.arange(groups, dtype=jnp.int32)
    tallies = jnp.sum((owners[:, None] == shard_ids[None, :]).astype(jnp.int32), axis=0)
    starts = jnp.cumsum(tallies) - tallies
    own_start = jnp.sum(
        jnp.where(sorted_owner[:, None] == shard_ids[None, :], starts[None, :], 0), axis=1
    )
    ranked = jnp.arange(count, dtype=jnp.int32) - own_start
    placed = sorted_owner * capacity + ranked
    position = jnp.zeros((count,), jnp.int32).at[sort_order].set(placed)
    outbound = jnp.full((groups * capacity,), -1, jnp.int32).at[position].set(row_keys)
    outbound = outbound.reshape(groups, capacity)
    flat_table = emb_table.reshape(slots_here * table_rows, row_width)
    inbound = lax.all_to_all(outbound, "emb", split_axis=0, concat_axis=0, tiled=True)
    gathered = jnp.take(flat_table, jnp.maximum(inbound, 0), axis=0).astype(jnp.bfloat16)
    returned = lax.all_to_all(gathered, "emb", split_axis=0, concat_axis=0, tiled=True)
    looked = returned.reshape(groups * capacity, row_width)[position]
    looked = looked.reshape(examples_here, slots_here, bag_size, row_width)
    in_bag = (
        lax.broadcasted_iota(jnp.int32, (examples_here, slots_here, bag_size), 2)
        < bag_len[:, :, None]
    )
    pooled = jnp.sum(jnp.where(in_bag[..., None], looked.astype(jnp.float32), 0.0), axis=2)
    features = pooled.reshape(examples_here, slots_here * row_width).astype(jnp.bfloat16)
    full_features = lax.all_gather(features, "sec", axis=1, tiled=True)
    pre_expert = jnp.dot(full_features, expert_w, preferred_element_type=jnp.float32)
    hidden = jax.nn.silu(pre_expert).astype(jnp.bfloat16)
    full_hidden = lax.all_gather(hidden, "sec", axis=1, tiled=True)
    pre_tower = jnp.dot(full_hidden, tower_w, preferred_element_type=jnp.float32)
    active = jax.nn.silu(pre_tower)
    section_share = jnp.sum(active * tower_out, axis=1)
    choose = (section_task[0] == jnp.arange(3, dtype=jnp.int32)).astype(jnp.float32)
    logits = lax.psum(section_share[:, None] * choose[None, :], "sec")
    chance = jax.nn.sigmoid(logits[:, :2])
    watch_err = (logits[:, 0] + logits[:, 1] + logits[:, 2] - watch)[:, None]
    residual = jnp.concatenate([chance - click_like + watch_err, watch_err], axis=1)
    task_back = jnp.sum(residual * choose[None, :], axis=1)
    head_grad = lax.psum(jnp.sum(active * task_back[:, None], axis=0)[None, :], "emb")
    tower_delta = (task_back[:, None] * tower_out * silu_slope(pre_tower)).astype(jnp.bfloat16)
    contract_rows = (((0,), (0,)), ((), ()))
    contract_cols = (((1,), (1,)), ((), ()))
    columns = full_hidden
    tower_grad = lax.psum_scatter(
        lax.dot_general(columns, tower_delta, contract_rows, preferred_element_type=jnp.float32),
        "emb",
        scatter_dimension=0,
        tiled=True,
    )
    hidden_part = lax.dot_general(
        tower_delta, tower_w, contract_cols, preferred_element_type=jnp.float32
    )
    hidden_grad = lax.psum_scatter(hidden_part, "sec", scatter_dimension=1, tiled=True)
    expert_delta = (hidden_grad * silu_slope(pre_expert)).astype(jnp.bfloat16)
    columns = full_features
    expert_grad = lax.psum_scatter(
        lax.dot_general(columns, expert_delta, contract_rows, preferred_element_type=jnp.float32),
        "emb",
        scatter_dimension=0,
        tiled=True,
    )
    feature_part = lax.dot_general(
        expert_delta, expert_w, contract_cols, preferred_element_type=jnp.float32
    )
    feature_grad = lax.psum_scatter(
        feature_part.astype(jnp.bfloat16), "sec", scatter_dimension=1, tiled=True
    ).astype(jnp.float32)
    feature_grad = feature_grad.reshape(examples_here, slots_here, 1, row_width)
    lookup_grad = jnp.where(in_bag[..., None], feature_grad, 0.0).reshape(count, row_width)
    outgoing = jnp.zeros((groups * capacity, row_width), jnp.float32).at[position].set(lookup_grad)
    incoming = lax.all_to_all(
        outgoing.reshape(groups, capacity, row_width).astype(jnp.bfloat16),
        "emb",
        split_axis=0,
        concat_axis=0,
        tiled=True,
    ).astype(jnp.float32)
    targets = jnp.where(inbound >= 0, inbound, slots_here * table_rows).reshape(-1)
    row_grad = jnp.zeros((slots_here * table_rows, row_width), jnp.float32)
    row_grad = row_grad.at[targets].add(incoming.reshape(-1, row_width), mode="drop")
    row_grad = row_grad.reshape(slots_here, table_rows, row_width)
    new_accum = emb_accum + row_grad * row_grad
    new_table = emb_table - learn_rate * row_grad / jnp.sqrt(new_accum)
    return (new_table, new_accum, expert_grad, tower_grad, head_grad)


def solution(mesh):
    placed = (
        P("sec", "emb", None),
        P("sec", "emb", None),
        P("emb", "sec", None),
        P("emb", "sec"),
        P(None, "sec"),
        P(None, "sec"),
        P("sec", None),
        P("sec"),
        P("emb", None),
        P("emb"),
    )
    return jax.shard_map(
        body,
        mesh=mesh,
        in_specs=placed,
        out_specs=(
            P("sec", "emb", None),
            P("sec", "emb", None),
            P("emb", "sec"),
            P("emb", "sec"),
            P("sec", None),
        ),
        check_vma=False,
    )
```

profile of v0, /device:TPU:1, one launch (start us, length us, event | category | flops | bytes accessed | tf_op | source)
XLA Modules:
  0.0 609.6 jit_solution(10699365723525561234)
XLA Ops:
  9.2 5.8 sort.17
  15.0 23.0 %gather_fusion = s32[4096]{0:T(1024)S(1)} fusion(s32[4096]{0:T(1024)S(1)} %reshape.150, s32[4096]{0:T(1024)S(1)} %get-tuple-element.45), kind=kCustom, calls=%fused_computation | custom fusion | bytes 49152 | tf_op jit(solution)/shard_map/gather | solution.py:35
  38.6 15.5 %scatter_custom_fusion = s32[4096]{0:T(1024)S(1)} fusion(s32[4096]{0:T(1024)S(1)} %get-tuple-element.46, s32[4096]{0:T(1024)S(1)} %subtract_add_fusion, s32[]{:T(128)} %constant.42.clone.1), kind=kCustom, calls=%fused_computation.54 | custom fusion | bytes 16388 | tf_op jit(solution)/shard_map/scatter | solution.py:44
  55.1 16.1 %scatter_custom_fusion.1 = s32[8192]{0:T(1024)} fusion(s32[4096]{0:T(1024)S(1)} %get-tuple-element.42, s32[4096]{0:T(1024)S(1)} %reshape.198, s32[]{:T(128)} %constant.35.clone.1), kind=kCustom, calls=%fused_computation.48 | custom fusion | bytes 32772 | tf_op jit(solution)/shard_map/scatter | solution.py:45
  71.2 13.0 %all-to-all-start = ((s32[64,1,128]{2,1,0:T(1,128)}), s32[64,1,128]{2,1,0:T(1,128)S(1)}, u32[]{:S(2)}, u32[]{:S(2)}) async-start(s32[64,1,128]{2,1,0:T(1,128)} %bitcast.1), calls=%async_computation | async-start | bytes 65536 | tf_op jit(solution)/shard_map/all_to_all | solution.py:48
  85.9 7.5 %all-to-all-done = s32[64,1,128]{2,1,0:T(1,128)S(1)} async-done(((s32[64,1,128]{2,1,0:T(1,128)}), s32[64,1,128]{2,1,0:T(1,128)S(1)}, u32[]{:S(2)}, u32[]{:S(2)}) %all-to-all-start) | async-done | bytes 32800 | tf_op jit(solution)/shard_map/all_to_all | solution.py:48
  93.4 29.2 %gather_fusion.1 = bf16[8192,64]{1,0:T(8,128)(2,1)} fusion(bf16[4096,64]{1,0:T(8,128)(2,1)S(1)} %bitcast.49, s32[8192]{0:T(1024)S(1)} %bitcast_clamp_fusion), kind=kCustom, calls=%fused_computation.1 | custom fusion | bytes 2129920 | tf_op jit(solution)/shard_map/jit(_take)/gather | solution.py:49
  126.0 4.8 all-to-all-start.1
  131.3 28.0 %all-to-all-done.1 = bf16[64,128,64]{1,2,0:T(8,128)(2,1)S(1)} async-done(((bf16[64,128,64]{1,2,0:T(8,128)(2,1)}), bf16[64,128,64]{1,2,0:T(8,128)(2,1)S(1)}, u32[]{:S(2)}, u32[]{:S(2)}) %all-to-all-start.1) | async-done | bytes 1048608 | tf_op jit(solution)/shard_map/all_to_all | solution.py:50
  161.2 12.9 %gather_fusion.2 = bf16[4096,64]{1,0:T(8,128)(2,1)S(1)} fusion(bf16[8192,64]{1,0:T(8,128)(2,1)} %bitcast.50, s32[4096]{0:T(1024)S(1)} %get-tuple-element.41), kind=kCustom, calls=%fused_computation.2 | custom fusion | bytes 1064960 | tf_op jit(solution)/shard_map/gather | solution.py:51
  174.1 5.0 fusion
  179.1 2.0 copy.107
  181.4 22.7 %all-gather.3.cloned.1.call-done = bf16[256,2048]{0,1:T(8,128)(2,1)} async-done(((bf16[256,512]{0,1:T(8,128)(2,1)}), bf16[256,2048]{0,1:T(8,128)(2,1)}) %all-gather.3.cloned.1.call-update) | async-done | bytes 1048592 | tf_op jit(solution)/shard_map/all_gather | solution.py:59
  204.1 2.7 multiply_convert_fusion.2
  207.5 26.3 %all-gather.5.cloned.1.call-done = bf16[256,2048]{1,0:T(8,128)(2,1)} async-done(((bf16[256,512]{1,0:T(8,128)(2,1)}), bf16[256,2048]{1,0:T(8,128)(2,1)}) %all-gather.5.cloned.1.call-update) | async-done | bytes 1048592 | tf_op jit(solution)/shard_map/all_gather | solution.py:62
  233.9 2.8 multiply_reduce_fusion.1
  236.7 7.3 %psum.14 = f32[256,3]{0,1:T(4,128)S(1)} all-reduce(f32[256,3]{0,1:T(4,128)S(1)} %broadcast_multiply_fusion.1), channel_id=1, replica_groups=mesh['emb'=64,'sec'=4] {'sec'}, use_global_device_ids=true, to_apply=%region_8.9 | all-reduce | flops 768 | bytes 6144 | tf_op jit(solution)/shard_map/psum | solution.py:67
  244.2 3.8 fusion.20
  248.1 34.6 %reduce-scatter.5.cloned.1.call-done = f32[256,512]{1,0:T(8,128)} async-done(((f32[256,2048]{1,0:T(8,128)}), f32[256,512]{1,0:T(8,128)}) %reduce-scatter.5.cloned.1.call-update) | async-done | bytes 524304 | tf_op jit(solution)/shard_map/reduce_scatter | solution.py:86
  286.4 3.9 fusion.19
  291.5 3.6 fusion.21
  295.8 15.1 %reduce-scatter.7.cloned.1.call-done = bf16[256,512]{1,0:T(8,128)(2,1)} async-done(((bf16[256,2048]{1,0:T(8,128)(2,1)}), bf16[256,512]{1,0:T(8,128)(2,1)}) %reduce-scatter.7.cloned.1.call-update) | async-done | bytes 262160 | tf_op jit(solution)/shard_map/reduce_scatter | solution.py:98
  314.2 2.1 broadcast_in_dim.116
  316.3 15.5 %scatter_custom_fusion.2 = f32[8192,64]{1,0:T(8,128)} fusion(s32[4096]{0:T(1024)} %copy-done.9, f32[4096,64]{1,0:T(8,128)} %bitcast.51, f32[]{:T(128)} %constant.34.clone.1, pred[4096]{0:T(1024)(128)(4,1)S(1)} %lt.52), kind=kCustom, calls=%fused_computation.10 | custom fusion | flops 262144 | bytes 4199424 | tf_op jit(solution)/shard_map/scatter | solution.py:103
  331.9 3.8 convert_element_type.56
  335.7 2.7 copy.110
  338.4 12.0 %all-to-all-start.2 = ((bf16[64,128,64]{1,2,0:T(8,128)(2,1)}), bf16[64,128,64]{1,2,0:T(8,128)(2,1)S(1)}, u32[]{:S(2)}, u32[]{:S(2)}) async-start(bf16[64,128,64]{1,2,0:T(8,128)(2,1)} %copy.110), calls=%async_computation.4 | async-start | bytes 2097152 | tf_op jit(solution)/shard_map/all_to_all | solution.py:104
  351.7 142.1 %psum.15 = f32[1,512]{1,0:T(1,128)} all-reduce(f32[1,512]{1,0:T(1,128)S(1)} %bitcast.64), channel_id=1, replica_groups=mesh['emb'=64,'sec'=4] {'emb'}, use_global_device_ids=true, to_apply=%region_17.18 | all-reduce | flops 512 | bytes 4096 | tf_op jit(solution)/shard_map/psum | solution.py:72
  493.8 2.4 copy.120
  496.2 45.8 %scatter_custom_fusion.3 = f32[4096,64]{1,0:T(8,128)} fusion(s32[8192]{0:T(1024)S(1)} %bitcast.62, f32[8192,64]{1,0:T(8,128)} %bitcast.55, f32[]{:T(128)} %constant.34.clone.1), kind=kCustom, calls=%fused_computation.22 | custom fusion | flops 524288 | bytes 1049088 | tf_op jit(solution)/shard_map/scatter-add | solution.py:113
  542.0 2.2 copy.113
  550.5 52.3 %reduce-scatter.9.cloned.1.call-done = f32[32,512]{1,0:T(8,128)} async-done(((f32[2048,512]{1,0:T(8,128)}), f32[32,512]{1,0:T(8,128)}) %reduce-scatter.9.cloned.1.call-update) | async-done | bytes 65552 | tf_op jit(solution)/shard_map/reduce_scatter | solution.py:89
  (85 shorter events, 28.0 us)
Async XLA Ops:
  7.2 196.9 %copy-start = (bf16[2048,512]{1,0:T(8,128)(2,1)S(1)}, bf16[2048,512]{1,0:T(8,128)(2,1)}, u32[]{:S(2)}) copy-start(bf16[2048,512]{1,0:T(8,128)(2,1)} %param.14) | copy-start | bytes 6291460
  54.2 31.7 %copy-start.9 = (s32[4096]{0:T(1024)}, s32[4096]{0:T(1024)S(1)}, u32[]{:S(2)}) copy-start(s32[4096]{0:T(1024)S(1)} %get-tuple-element.42) | copy-start | bytes 49156
  71.2 22.2 %all-to-all-start = ((s32[64,1,128]{2,1,0:T(1,128)}), s32[64,1,128]{2,1,0:T(1,128)S(1)}, u32[]{:S(2)}, u32[]{:S(2)}) async-start(s32[64,1,128]{2,1,0:T(1,128)} %bitcast.1), calls=%async_computation | async-start | bytes 65536 | tf_op jit(solution)/shard_map/all_to_all | solution.py:48
  93.4 29.3 %copy-start.7 = (s32[64,1,128]{2,1,0:T(1,128)}, s32[64,1,128]{2,1,0:T(1,128)S(1)}, u32[]{:S(2)}) copy-start(s32[64,1,128]{2,1,0:T(1,128)S(1)} %all-to-all-done) | copy-start | bytes 98308
  124.7 6.2 %copy-start.10 = (s32[256,8]{0,1:T(8,128)S(1)}, s32[256,8]{0,1:T(8,128)}, u32[]{:S(2)}) copy-start(s32[256,8]{0,1:T(8,128)} %param.13) | copy-start | bytes 24580
  126.0 33.3 %all-to-all-start.1 = ((bf16[64,128,64]{1,2,0:T(8,128)(2,1)}), bf16[64,128,64]{1,2,0:T(8,128)(2,1)S(1)}, u32[]{:S(2)}, u32[]{:S(2)}) async-start(bf16[64,128,64]{1,2,0:T(8,128)(2,1)} %select_convert_fusion), calls=%async_computation.1 | async-start | bytes 2097152 | tf_op jit(solution)/shard_map/all_to_all | solution.py:50
  130.8 73.3 %all-gather.3.cloned.1.call-start = ((), (), s32[]{:S(2)}) async-start(), calls=%async_computation.7 | async-start | bytes 1310720 | tf_op jit(solution)/shard_map/all_gather | solution.py:59
  181.2 52.7 %copy-start.11 = (f32[1,512]{1,0:T(1,128)S(1)}, f32[1,512]{1,0:T(1,128)}, u32[]{:S(2)}) copy-start(f32[1,512]{1,0:T(1,128)} %param.16) | copy-start | bytes 6148
  181.2 52.7 %all-gather.5.cloned.1.call-start = ((), (), s32[]{:S(2)}) async-start(), calls=%async_computation.8 | async-start | bytes 1310720 | tf_op jit(solution)/shard_map/all_gather | solution.py:62
  206.8 75.8 %reduce-scatter.5.cloned.1.call-start = ((), (), s32[]{:S(2)}) async-start(), calls=%async_computation.9 | async-start | bytes 2621440 | tf_op jit(solution)/shard_map/reduce_scatter | solution.py:86
  233.9 10.2 %copy-start.13 = (f32[256]{0:T(256)S(1)}, f32[256]{0:T(256)}, u32[]{:S(2)}) copy-start(f32[256]{0:T(256)} %param.19) | copy-start | bytes 3076
  233.9 10.2 %copy-start.12 = (f32[256,2]{0,1:T(2,128)S(1)}, f32[256,2]{0,1:T(2,128)}, u32[]{:S(2)}) copy-start(f32[256,2]{0,1:T(2,128)} %param.18) | copy-start | bytes 6148
  236.7 11.3 %copy-start.5 = (f32[256,512]{1,0:T(8,128)}, f32[256,512]{1,0:T(8,128)S(1)}, u32[]{:S(2)}) copy-start(f32[256,512]{1,0:T(8,128)S(1)} %get-tuple-element.50) | copy-start | bytes 1572868
  248.0 62.9 %reduce-scatter.7.cloned.1.call-start = ((), (), s32[]{:S(2)}) async-start(), calls=%async_computation.10 | async-start | bytes 1310720 | tf_op jit(solution)/shard_map/reduce_scatter | solution.py:98
  283.9 0.7 copy-start.4
  284.6 1.8 copy-start.2
  286.3 264.1 %reduce-scatter.11.cloned.1.call-start = ((), (), s32[]{:S(2)}) async-start(), calls=%async_computation.12 | async-start | bytes 4259840 | tf_op jit(solution)/shard_map/reduce_scatter | solution.py:77
  290.3 1.2 copy-start.3
  290.3 312.5 %reduce-scatter.9.cloned.1.call-start = ((), (), s32[]{:S(2)}) async-start(), calls=%async_computation.11 | async-start | bytes 4259840 | tf_op jit(solution)/shard_map/reduce_scatter | solution.py:89
  335.7 14.7 %copy-start.8 = (s32[64,1,128]{2,1,0:T(1,128)S(1)}, s32[64,1,128]{2,1,0:T(1,128)}, u32[]{:S(2)}) copy-start(s32[64,1,128]{2,1,0:T(1,128)} %copy-done.7) | copy-start | bytes 98308
  338.4 155.4 %all-to-all-start.2 = ((bf16[64,128,64]{1,2,0:T(8,128)(2,1)}), bf16[64,128,64]{1,2,0:T(8,128)(2,1)S(1)}, u32[]{:S(2)}, u32[]{:S(2)}) async-start(bf16[64,128,64]{1,2,0:T(8,128)(2,1)} %copy.110), calls=%async_computation.4 | async-start | bytes 2097152 | tf_op jit(solution)/shard_map/all_to_all | solution.py:104
  544.4 1.3 copy-start.1
  544.4 1.5 copy-start.6
Sparse Core Ops, SparseCore 0:
  181.3 22.7 all-gather.2
  206.9 26.8 all-gather.4
  248.1 34.4 reduce-scatter.4
  286.5 24.3 reduce-scatter.6
  315.4 139.9 reduce-scatter.10
  460.5 142.2 reduce-scatter.8
where the time goes:
time: 615 us; the launch traced here: 610 us
  waiting for transfers between devices  187 us (30%)
  blocking collectives  149 us (24%)
  local copies, waits for them, and re-layouts  126 us (20%)
  other arithmetic  83.5 us (14%)
  starting transfers between devices  30.1 us (5%)
  matrix products  18.5 us (3%)
  between operations  15.1 us (2%)
    psum x1, blocking collectives, body(): lax.psum(jnp.sum(active * task_back[:, None], axis=0)[None, :], 'emb')  142 us
    reduce_scatter x1, waiting for transfers between devices, body(): lax.psum_scatter(lax.dot_general(columns, expert_delta, contract_rows, pr...  52.3 us
    scatter-add x1, other arithmetic, body(): row_grad.at[targets].add(incoming.reshape(-1, row_width), mode='drop')  45.8 us
    reduce_scatter x1, waiting for transfers between devices, body(): lax.psum_scatter(hidden_part, 'sec', scatter_dimension=1, tiled=True)  34.6 us
    gather x2, local copies, waits for them, and re-layouts, body(): jnp.take(flat_table, jnp.maximum(inbound, 0), axis=0).astype(jnp.bfloat16)  31.2 us
    all_to_all x1, waiting for transfers between devices, body(): lax.all_to_all(gathered, 'emb', split_axis=0, concat_axis=0, tiled=True)  28 us
    all_gather x1, waiting for transfers between devices, body(): full_hidden = lax.all_gather(hidden, 'sec', axis=1, tiled=True)  26.3 us
    gather x1, local copies, waits for them, and re-layouts, body(): sorted_owner = owners[sort_order]  23 us
  transfers between devices with their start and end apart: 9, of which 7 were waited for; matrix products, arithmetic and copies ran while one was open for 16% of the time, Pallas kernels for 0%

commit v1 on v0

v1 whole, which is shorter than its diff:
```python
import jax
import jax.numpy as jnp
from jax import lax
from jax.experimental import pallas as pl
from jax.experimental.pallas import tpu as pltpu
from jax.sharding import PartitionSpec as P

MESH = pl.DeviceIdType.MESH
learn_rate = 0.2
f32 = jnp.float32
bf16 = jnp.bfloat16
i32 = jnp.int32

EMB = 64
SEC = 4
XS = 4
ZS = 8
CAP = 128
DIM = 64
SLOTS = 8
BATCH = 256
ROWS = 512
WIDE = 512


def mm(a, b):
    return lax.dot_general(a, b, (((1,), (0,)), ((), ())), preferred_element_type=f32)


def mm_nt(a, b):
    return lax.dot_general(a, b, (((1,), (1,)), ((), ())), preferred_element_type=f32)


def silu_slope(value):
    logistic = jax.nn.sigmoid(value)
    return logistic * (1.0 + value * (1.0 - logistic))


def hot(size, keys):
    rows = lax.broadcasted_iota(i32, (size, keys.shape[1]), 0)
    return jnp.where(rows == keys, 1.0, 0.0).astype(bf16)


def remote(src, dst, send, recv, **where):
    return pltpu.make_async_remote_copy(
        src_ref=src, dst_ref=dst, send_sem=send, recv_sem=recv, device_id=where, device_id_type=MESH
    )


def greet(emb, sec=None):
    barrier = pltpu.get_barrier_semaphore()

    @pl.loop(1, EMB)
    def _(d):
        pl.semaphore_signal(barrier, inc=1, device_id={"emb": lax.rem(emb + d, EMB)}, device_id_type=MESH)

    if sec is not None:
        for d in range(1, SEC):
            pl.semaphore_signal(barrier, inc=1, device_id={"sec": lax.rem(sec + d, SEC)}, device_id_type=MESH)


def meet(sec=None):
    pl.semaphore_wait(pltpu.get_barrier_semaphore(), EMB - 1 + (0 if sec is None else SEC - 1))


def route(ids_ref, ob, pos):
    before = lax.broadcasted_iota(i32, (BATCH, BATCH), 0)
    after = lax.broadcasted_iota(i32, (BATCH, BATCH), 1)
    upper = jnp.where(before < after, 1.0, 0.0).astype(bf16)
    shard_row = lax.broadcasted_iota(i32, (EMB, BATCH), 0)
    rank_row = lax.broadcasted_iota(i32, (CAP, BATCH), 0)
    carry = jnp.zeros((EMB, 1), f32)
    total = jnp.zeros((EMB, 2 * CAP), f32)
    for q in range(2 * SLOTS):
        ids = ids_ref[q : q + 1, :]
        owner = ids >> 9
        key = (ids & (ROWS - 1)) + ((q // 2) * ROWS + 1)
        owned = jnp.where(shard_row == owner, 1.0, 0.0)
        owned_b = owned.astype(bf16)
        prefix = mm(owned_b, upper) + carry
        rank = jnp.sum(owned * prefix, axis=0, keepdims=True).astype(i32)
        carry = carry + jnp.sum(owned, axis=1, keepdims=True)
        pos[q] = owner * CAP + rank
        ranked = rank_row == rank
        high = jnp.where(ranked, (key >> 6).astype(f32), 0.0).astype(bf16)
        low = jnp.where(ranked, (key & 63).astype(f32), 0.0).astype(bf16)
        total = total + mm_nt(owned_b, jnp.concatenate([high, low], axis=0))
    keys = (total[:, :CAP] * 64.0 + total[:, CAP:]).astype(i32) - 1
    for s in range(EMB):
        ob[s] = keys[s : s + 1, :]


def lookup_kernel(
    ids_ref, bag_ref, table_ref, feat_ref, pos_ref, key_ref,
    ob, ib, out_rows, in_rows, wide_rows, tb, id_send, id_recv, row_send, row_recv,
):
    me = lax.axis_index("emb")
    greet(me)
    route(ids_ref, ob, pos_ref)
    meet()

    @pl.loop(1, EMB)
    def _(d):
        peer = lax.rem(me + d, EMB)
        remote(ob.at[peer], ib.at[me], id_send.at[peer], id_recv.at[me], emb=peer).start()

    ib[me] = ob[me]
    tb[...] = table_ref[...].astype(bf16)

    @pl.loop(0, EMB // 2)
    def _(t):
        a = lax.rem(me + EMB - 2 * t, EMB)
        b = lax.rem(me + EMB - 2 * t - 1, EMB)

        @pl.when(t > 0)
        def _():
            remote(ob.at[a], ib.at[a], id_send.at[a], id_recv.at[a], emb=a).wait_recv()

        remote(ob.at[b], ib.at[b], id_send.at[b], id_recv.at[b], emb=b).wait_recv()
        keys = jnp.concatenate([ib[a], ib[b]], axis=1)
        slot = keys >> 9
        picked = mm(tb[...], hot(ROWS, keys & (ROWS - 1)))
        rows = jnp.zeros((DIM, 2 * CAP), f32)
        for s in range(SLOTS):
            rows = rows + jnp.where(slot == s, picked[s * DIM : (s + 1) * DIM], 0.0)
        rows = rows.astype(bf16)
        out_rows[a] = rows[:, :CAP]
        out_rows[b] = rows[:, CAP:]

        @pl.when(t == 0)
        def _():
            in_rows[me] = rows[:, :CAP]

        @pl.when(t > 0)
        def _():
            remote(out_rows.at[a], in_rows.at[me], row_send.at[a], row_recv.at[me], emb=a).start()

        remote(out_rows.at[b], in_rows.at[me], row_send.at[b], row_recv.at[me], emb=b).start()

    @pl.loop(1, EMB)
    def _(d):
        peer = lax.rem(me + d, EMB)
        remote(ob.at[peer], ib.at[peer], id_send.at[peer], id_recv.at[peer], emb=peer).wait_send()
        remote(out_rows.at[peer], in_rows.at[peer], row_send.at[peer], row_recv.at[peer], emb=peer).wait_recv()

    for h in range(8):
        wide_rows[:, h * CAP : (h + 1) * CAP] = in_rows[h * 8 : (h + 1) * 8].reshape(8 * DIM, CAP)

    @pl.loop(0, SLOTS)
    def _(s):
        pooled = jnp.zeros((DIM, BATCH), f32)
        for k in range(2):
            place = pos_ref[2 * s + k]
            shard = place >> 7
            low = jnp.where(bag_ref[s] > k, shard & 7, -1)
            picked = mm(wide_rows[...], hot(8 * CAP, (shard >> 3) * CAP + (place & (CAP - 1))))
            for g in range(8):
                pooled = pooled + jnp.where(low == g, picked[g * DIM : (g + 1) * DIM], 0.0)
        feat_ref[pl.ds(pl.multiple_of(s * DIM, DIM), DIM), :] = pooled.astype(bf16)

    key_ref[...] = ib[...]

    @pl.loop(1, EMB)
    def _(d):
        peer = lax.rem(me + d, EMB)
        remote(out_rows.at[peer], in_rows.at[peer], row_send.at[peer], row_recv.at[peer], emb=peer).wait_send()


def step_kernel(
    task_ref, feat_ref, pos_ref, key_ref, bag_ref, expert_ref, tower_ref, out_row_ref, out_col_ref, click_ref, watch_ref,
    grad_ref, expert_grad_ref, tower_grad_ref, head_ref,
    feats, hiddens, expert_t, tower_t, pre_e, pre_t, shares, part_out, part_in, whole, own_part,
    core_out, core_in, x_out, x_in, z_out, z_in, head_core, head_x, head_z,
    spread, out_grads, in_grads,
    feat_sem, hidden_sem, share_sem, part_sem, core_sem, x_sem, z_sem, hcore_sem, hx_sem, hz_sem, grad_send, grad_recv,
):
    me = lax.axis_index("emb")
    sec = lax.axis_index("sec")
    core = lax.rem(me, 2)
    z = lax.rem(lax.div(me, 2), ZS)
    x = lax.div(me, 2 * ZS)
    partner = me + 1 - 2 * core
    greet(me, sec)
    feats[sec] = feat_ref[...]
    meet(sec)

    def across(d):
        return lax.rem(sec + d, SEC)

    def spread_out(buffer, sems):
        for d in (2, 1, 3):
            remote(buffer.at[sec], buffer.at[sec], sems.at[0, d], sems.at[1, sec], sec=across(d)).start()

    def arrive(buffer, sems, d):
        remote(buffer.at[sec], buffer.at[across(d)], sems.at[0, d], sems.at[1, across(d)], sec=across(d)).wait_recv()

    def left(buffer, sems):
        for d in (2, 1, 3):
            remote(buffer.at[sec], buffer.at[sec], sems.at[0, d], sems.at[1, sec], sec=across(d)).wait_send()

    def rows_of(r):
        return pl.ds(pl.multiple_of(r * WIDE, WIDE), WIDE)

    spread_out(feats, feat_sem)

    @pl.loop(0, SEC)
    def _(r):
        expert_t[r] = expert_ref[rows_of(r), :].T
        tower_t[r] = tower_ref[rows_of(r), :].T

    pre_e[...] = mm(expert_t[sec], feats[sec])
    for d in (1, 3, 2):
        arrive(feats, feat_sem, d)
        pre_e[...] += mm(expert_t[across(d)], feats[across(d)])
    hiddens[sec] = jax.nn.silu(pre_e[...]).astype(bf16)
    spread_out(hiddens, hidden_sem)
    pre_t[...] = mm(tower_t[sec], hiddens[sec])
    for d in (1, 3, 2):
        arrive(hiddens, hidden_sem, d)
        pre_t[...] += mm(tower_t[across(d)], hiddens[across(d)])
    active = jax.nn.silu(pre_t[...])
    share = jnp.sum(active * out_col_ref[...], axis=0, keepdims=True)
    chosen = jnp.where(lax.broadcasted_iota(i32, (8, BATCH), 0) == task_ref[0], 1.0, 0.0)
    shares[sec] = share * chosen
    spread_out(shares, share_sem)
    slope = out_col_ref[...] * silu_slope(pre_t[...])
    for d in (1, 3, 2):
        arrive(shares, share_sem, d)
    logits = (shares[0] + shares[1]) + (shares[2] + shares[3])
    err = logits[0:1] + logits[1:2] + logits[2:3] - watch_ref[...]
    chance = jax.nn.sigmoid(logits[0:2]) - click_ref[...] + err
    back = chance[0:1] * chosen[0:1] + chance[1:2] * chosen[1:2] + err * chosen[2:3]
    tower_delta = (back * slope).astype(bf16)

    def part_copy(n, d, at):
        return remote(part_out.at[n, d], part_in.at[n, at], part_sem.at[n, 0, d], part_sem.at[n, 1, at], sec=across(d))

    def part(n, weights_ref, delta):
        for d in (2, 1, 3):
            peer = across(d)
            part_out[n, d] = mm(weights_ref[rows_of(peer), :], delta).astype(bf16)
            part_copy(n, d, sec).start()
        own_part[...] = mm(weights_ref[rows_of(sec), :], delta)

    def part_sum(n):
        for d in (1, 3, 2):
            part_copy(n, d, across(d)).wait_recv()
            own_part[...] += part_in[n, across(d)].astype(f32)
        for d in (2, 1, 3):
            part_copy(n, d, sec).wait_send()

    def core_copy(n):
        return remote(core_out.at[n], core_in.at[n], core_sem.at[0, n], core_sem.at[1, n], emb=partner)

    def weight_grad(n, source, delta):
        @pl.loop(0, SEC)
        def _(r):
            whole[n, pl.ds(r * 16, 16)] = mm_nt(source[r], delta).reshape(16, 32, WIDE)

        @pl.loop(0, 32)
        def _(j):
            core_out[n, j] = whole[n, 2 * j + 1 - core].astype(bf16)

        core_copy(n).start()

    def x_copy(n, d):
        to = lax.rem(x + d, XS)
        return remote(
            x_out.at[n, to], x_in.at[n, x], x_sem.at[n, 0, d], x_sem.at[n, 1, x], emb=(to * ZS + z) * 2 + core
        )

    def x_arrive(n, d):
        to = lax.rem(x + d, XS)
        return remote(
            x_out.at[n, to], x_in.at[n, to], x_sem.at[n, 0, d], x_sem.at[n, 1, to], emb=(to * ZS + z) * 2 + core
        )

    def z_copy(n, d):
        to = lax.rem(z + d, ZS)
        return remote(
            z_out.at[n, to], z_in.at[n, z], z_sem.at[n, 0, d], z_sem.at[n, 1, z], emb=(x * ZS + to) * 2 + core
        )

    def z_arrive(n, d):
        to = lax.rem(z + d, ZS)
        return remote(
            z_out.at[n, to], z_in.at[n, to], z_sem.at[n, 0, d], z_sem.at[n, 1, to], emb=(x * ZS + to) * 2 + core
        )

    def core_sum(n):
        core_copy(n).wait()

        @pl.loop(0, 32)
        def _(j):
            value = whole[n, 2 * j + core] + core_in[n, j].astype(f32)
            whole[n, 2 * j + core] = value
            x_out[n, lax.div(j, ZS), lax.rem(j, ZS)] = value.astype(bf16)

        for d in (2, 1, 3):
            x_copy(n, d).start()

    def x_sum(n):
        for d in (1, 3, 2):
            x_arrive(n, d).wait_recv()

        @pl.loop(0, ZS)
        def _(j):
            at = 2 * (x * ZS + j) + core
            value = whole[n, at]
            for d in range(1, XS):
                value = value + x_in[n, lax.rem(x + d, XS), j].astype(f32)
            whole[n, at] = value
            z_out[n, j] = value.astype(bf16)

        for d in range(1, ZS):
            z_copy(n, d).start()

    def z_sum(n, result):
        for d in range(1, ZS):
            z_arrive(n, d).wait_recv()
        value = whole[n, me]
        for d in range(1, ZS):
            value = value + z_in[n, lax.rem(z + d, ZS)].astype(f32)
        result[...] = value
        for d in range(1, XS):
            x_copy(n, d).wait_send()
        for d in range(1, ZS):
            z_copy(n, d).wait_send()

    def hc_copy():
        return remote(head_core.at[0], head_core.at[1], hcore_sem.at[0], hcore_sem.at[1], emb=partner)

    def hx_copy(d, at):
        to = lax.rem(x + d, XS)
        return remote(head_x.at[x], head_x.at[at], hx_sem.at[0, d], hx_sem.at[1, at], emb=(to * ZS + z) * 2 + core)

    def hz_copy(d, at):
        to = lax.rem(z + d, ZS)
        return remote(head_z.at[z], head_z.at[at], hz_sem.at[0, d], hz_sem.at[1, at], emb=(x * ZS + to) * 2 + core)

    part(0, tower_ref, tower_delta)
    head_core[0] = lax.dot_general(
        back, active, (((1,), (1,)), ((), ())), preferred_element_type=f32, precision=lax.Precision.HIGHEST
    )
    hc_copy().start()
    weight_grad(0, hiddens, tower_delta)
    hc_copy().wait()
    head_x[x] = head_core[0] + head_core[1]
    for d in range(1, XS):
        hx_copy(d, x).start()
    core_sum(0)
    left(feats, feat_sem)
    left(hiddens, hidden_sem)
    left(shares, share_sem)
    for d in range(1, XS):
        hx_copy(d, lax.rem(x + d, XS)).wait_recv()
    head_z[z] = (head_x[0] + head_x[1]) + (head_x[2] + head_x[3])
    for d in range(1, ZS):
        hz_copy(d, z).start()

    part_sum(0)
    expert_delta = (own_part[...] * silu_slope(pre_e[...])).astype(bf16)
    part(1, expert_ref, expert_delta)
    weight_grad(1, feats, expert_delta)
    x_sum(0)
    core_sum(1)
    part_sum(1)

    @pl.loop(0, SLOTS)
    def _(s):
        grad = own_part[pl.ds(pl.multiple_of(s * DIM, DIM), DIM), :]
        for k in range(2):
            low = jnp.where(bag_ref[s] > k, (pos_ref[2 * s + k] >> 7) & 7, -1)
            for g in range(8):
                spread[2 * s + k, g * DIM : (g + 1) * DIM, :] = jnp.where(low == g, grad, 0.0).astype(bf16)

    @pl.loop(0, 4)
    def _(t):
        pair = lax.rem(lax.div(me, 16) + t, 4)

        def add(q, total):
            place = pos_ref[q]
            key = ((place >> 10) - 2 * pair) * CAP + (place & (CAP - 1))
            return total + mm_nt(spread[q], hot(2 * CAP, key))

        total = lax.fori_loop(0, 2 * SLOTS, add, jnp.zeros((8 * DIM, 2 * CAP), f32)).astype(bf16)
        for h in range(2):
            for g in range(8):
                peer = (2 * pair + h) * 8 + g
                out_grads[peer] = total[g * DIM : (g + 1) * DIM, h * CAP : (h + 1) * CAP]

                @pl.when(peer != me)
                def _():
                    remote(
                        out_grads.at[peer], in_grads.at[me], grad_send.at[peer], grad_recv.at[me], emb=peer
                    ).start()

                @pl.when(peer == me)
                def _():
                    in_grads[me] = total[g * DIM : (g + 1) * DIM, h * CAP : (h + 1) * CAP]

    x_sum(1)
    z_sum(0, tower_grad_ref)
    for d in range(1, ZS):
        hz_copy(d, lax.rem(z + d, ZS)).wait_recv()
    head = head_z[0]
    for j in range(1, ZS):
        head = head + head_z[j]
    head_ref[...] = head

    @pl.loop(1, EMB)
    def _(d):
        peer = lax.rem(me + d, EMB)
        remote(out_grads.at[peer], in_grads.at[peer], grad_send.at[peer], grad_recv.at[peer], emb=peer).wait_recv()

    grad_ref[...] = jnp.zeros((WIDE, ROWS), f32)

    @pl.loop(0, EMB // 2)
    def _(t):
        keys = jnp.concatenate([key_ref[2 * t], key_ref[2 * t + 1]], axis=1)
        slot = keys >> 9
        grads = jnp.concatenate([in_grads[2 * t], in_grads[2 * t + 1]], axis=1).astype(f32)
        wide = jnp.concatenate([jnp.where(slot == s, grads, 0.0) for s in range(SLOTS)], axis=0).astype(bf16)
        grad_ref[...] += mm_nt(wide, hot(ROWS, keys & (ROWS - 1)))

    z_sum(1, expert_grad_ref)
    for d in range(1, XS):
        hx_copy(d, x).wait_send()
    for d in range(1, ZS):
        hz_copy(d, z).wait_send()

    @pl.loop(1, EMB)
    def _(d):
        peer = lax.rem(me + d, EMB)
        remote(out_grads.at[peer], in_grads.at[peer], grad_send.at[peer], grad_recv.at[peer], emb=peer).wait_send()


def body(
    emb_table,
    emb_accum,
    slot_ids,
    bag_len,
    expert_w,
    tower_w,
    tower_out,
    section_task,
    click_like,
    watch,
):
    vmem = pl.BlockSpec(memory_space=pltpu.VMEM)
    dma = pltpu.SemaphoreType.DMA
    table = emb_table.transpose(0, 2, 1).reshape(SLOTS * DIM, ROWS)
    accum = emb_accum.transpose(0, 2, 1).reshape(SLOTS * DIM, ROWS)
    ids = slot_ids.transpose(1, 2, 0).reshape(2 * SLOTS, BATCH)
    bag = bag_len.T.reshape(SLOTS, 1, BATCH)
    features, places, keys = pl.pallas_call(
        lookup_kernel,
        out_shape=(
            jax.ShapeDtypeStruct((SLOTS * DIM, BATCH), bf16),
            jax.ShapeDtypeStruct((2 * SLOTS, 1, BATCH), i32),
            jax.ShapeDtypeStruct((EMB, 1, CAP), i32),
        ),
        in_specs=[vmem] * 3,
        out_specs=(vmem,) * 3,
        scratch_shapes=[
            pltpu.VMEM((EMB, 1, CAP), i32),
            pltpu.VMEM((EMB, 1, CAP), i32),
            pltpu.VMEM((EMB, DIM, CAP), bf16),
            pltpu.VMEM((EMB, DIM, CAP), bf16),
            pltpu.VMEM((8 * DIM, 8 * CAP), bf16),
            pltpu.VMEM((SLOTS * DIM, ROWS), bf16),
            dma((EMB,)),
            dma((EMB,)),
            dma((EMB,)),
            dma((EMB,)),
        ],
        compiler_params=pltpu.CompilerParams(collective_id=0, has_side_effects=True, vmem_limit_bytes=32 << 20),
    )(ids, bag, table)
    row_grad, expert_grad, tower_grad, head_grad = pl.pallas_call(
        step_kernel,
        out_shape=(
            jax.ShapeDtypeStruct((SLOTS * DIM, ROWS), f32),
            jax.ShapeDtypeStruct((32, WIDE), f32),
            jax.ShapeDtypeStruct((32, WIDE), f32),
            jax.ShapeDtypeStruct((1, WIDE), f32),
        ),
        in_specs=[pl.BlockSpec(memory_space=pltpu.SMEM)] + [vmem] * 10,
        out_specs=(vmem,) * 4,
        scratch_shapes=[
            pltpu.VMEM((SEC, WIDE, BATCH), bf16),
            pltpu.VMEM((SEC, WIDE, BATCH), bf16),
            pltpu.VMEM((SEC, WIDE, WIDE), bf16),
            pltpu.VMEM((SEC, WIDE, WIDE), bf16),
            pltpu.VMEM((WIDE, BATCH), f32),
            pltpu.VMEM((WIDE, BATCH), f32),
            pltpu.VMEM((SEC, 8, BATCH), f32),
            pltpu.VMEM((2, SEC, WIDE, BATCH), bf16),
            pltpu.VMEM((2, SEC, WIDE, BATCH), bf16),
            pltpu.VMEM((2, EMB, 32, WIDE), f32),
            pltpu.VMEM((WIDE, BATCH), f32),
            pltpu.VMEM((2, 32, 32, WIDE), bf16),
            pltpu.VMEM((2, 32, 32, WIDE), bf16),
            pltpu.VMEM((2, XS, ZS, 32, WIDE), bf16),
            pltpu.VMEM((2, XS, ZS, 32, WIDE), bf16),
            pltpu.VMEM((2, ZS, 32, WIDE), bf16),
            pltpu.VMEM((2, ZS, 32, WIDE), bf16),
            pltpu.VMEM((2, 1, WIDE), f32),
            pltpu.VMEM((XS, 1, WIDE), f32),
            pltpu.VMEM((ZS, 1, WIDE), f32),
            pltpu.VMEM((2 * SLOTS, 8 * DIM, BATCH), bf16),
            pltpu.VMEM((EMB, DIM, CAP), bf16),
            pltpu.VMEM((EMB, DIM, CAP), bf16),
            dma((2, SEC)),
            dma((2, SEC)),
            dma((2, SEC)),
            dma((2, 2, SEC)),
            dma((2, 2)),
            dma((2, 2, XS)),
            dma((2, 2, ZS)),
            dma((2,)),
            dma((2, XS)),
            dma((2, ZS)),
            dma((EMB,)),
            dma((EMB,)),
        ],
        compiler_params=pltpu.CompilerParams(collective_id=1, has_side_effects=True, vmem_limit_bytes=60 << 20),
    )(
        section_task,
        features,
        places,
        keys,
        bag,
        expert_w,
        tower_w,
        tower_out,
        tower_out.reshape(WIDE, 1),
        click_like.T,
        watch.reshape(1, BATCH),
    )
    new_accum = accum + row_grad * row_grad
    new_table = table - learn_rate * row_grad / jnp.sqrt(new_accum)

    def back(value):
        return value.reshape(SLOTS, DIM, ROWS).transpose(0, 2, 1)

    return (back(new_table), back(new_accum), expert_grad, tower_grad, head_grad)


def solution(mesh):
    placed = (
        P("sec", "emb", None),
        P("sec", "emb", None),
        P("emb", "sec", None),
        P("emb", "sec"),
        P(None, "sec"),
        P(None, "sec"),
        P("sec", None),
        P("sec"),
        P("emb", None),
        P("emb"),
    )
    return jax.shard_map(
        body,
        mesh=mesh,
        in_specs=placed,
        out_specs=(
            P("sec", "emb", None),
            P("sec", "emb", None),
            P("emb", "sec"),
            P("emb", "sec"),
            P("sec", None),
        ),
        check_vma=False,
    )
```

time: 615 us -> 174 us (0.28)
  waiting for transfers between devices: 187 us -> 0 us
  Pallas kernels: 0 us -> 161 us
  blocking collectives: 149 us -> 0 us
  local copies, waits for them, and re-layouts: 126 us -> 7.98 us
  other arithmetic: 83.5 us -> 2.88 us
  starting transfers between devices: 30.1 us -> 0 us
  matrix products: 18.5 us -> 0 us
  between operations: 15.1 us -> 1.35 us
    pallas_call x0 -> x2, Pallas kernels: none -> 161 us  [the longest x1 111 us: body(): pl.pallas_call(step_kernel, out_shape=(jax.ShapeDtypeStruct((SLOTS * DIM,...]
    psum x2 -> x0, blocking collectives: 149 us -> none  [the longest x1 142 us: body(): lax.psum(jnp.sum(active * task_back[:, None], axis=0)[None, :], 'emb')]
    reduce_scatter x4 -> x0, waiting for transfers between devices: 102 us -> none  [the longest x1 52.3 us: body(): lax.psum_scatter(lax.dot_general(columns, expert_delta, contract_rows, pr...]
    gather x4 -> x0, local copies, waits for them, and re-layouts: 67.1 us -> none  [the longest x2 31.2 us: body(): jnp.take(flat_table, jnp.maximum(inbound, 0), axis=0).astype(jnp.bfloat16)]
    all_gather x2 -> x0, waiting for transfers between devices: 49 us -> none  [the longest x1 26.3 us: body(): full_hidden = lax.all_gather(hidden, 'sec', axis=1, tiled=True)]
    scatter-add x1 -> x0, other arithmetic: 45.8 us -> none  [body(): row_grad.at[targets].add(incoming.reshape(-1, row_width), mode='drop')]
    all_to_all x3 -> x0, waiting for transfers between devices: 35.5 us -> none  [the longest x1 28 us: body(): lax.all_to_all(gathered, 'emb', split_axis=0, concat_axis=0, tiled=True)]
    scatter x2 -> x0, local copies, waits for them, and re-layouts: 31.6 us -> none  [the longest x1 16.1 us: body(): jnp.full((groups * capacity,), -1, jnp.int32).at[position].set(row_keys)]
  transfers between devices with their start and end apart: 9 -> 0, of which waited for: 7 -> 0; matrix products, arithmetic and copies ran while one was open for 16% -> 0% of each run, Pallas kernels for 0% -> 0%
where the time goes in v1:
time: 174 us
  Pallas kernels  161 us (93%)
  local copies, waits for them, and re-layouts  7.98 us (5%)
  other arithmetic  2.88 us (2%)
    pallas_call x1, Pallas kernels, body(): pl.pallas_call(step_kernel, out_shape=(jax.ShapeDtypeStruct((SLOTS * DIM,...  111 us
    pallas_call x1, Pallas kernels, body(): pl.pallas_call(lookup_kernel, out_shape=(jax.ShapeDtypeStruct((SLOTS * DI...  50.3 us
    unnamed x23, local copies, waits for them, and re-layouts  5 us

profile of v1, /device:TPU:1, one launch (start us, length us, event | category | flops | bytes accessed | tf_op | source)
XLA Modules:
  0.0 173.6 jit_solution(9159779063818813771)
XLA Ops:
  1.3 0.7 reshape.36.bag_ref
  2.0 0.0 copy-start.3
  2.0 0.7 reshape.35.ids_ref
  2.7 1.5 copy.15.out_col_ref
  4.3 0.0 copy-start
  4.3 1.2 copy-done
  5.5 50.3 %shard_map.137 = (bf16[512,256]{1,0:T(8,128)(2,1)S(1)}, s32[16,1,256]{2,1,0:T(1,128)S(1)}, s32[64,1,128]{2,1,0:T(1,128)S(1)}) custom-call(s32[16,256]{1,0:T(8,128)S(1)} %reshape.35.ids_ref, s32[8,1,256]{2,1,0:T(1,128)S(1)} %reshape.36.bag_ref, f32[512,512]{1,0:T(8,128)S(1)} %bitcast.20), custom_call_target="tpu_custom_call" | custom-call | tf_op jit(solution)/shard_map/pallas_call | solution.py:456
  55.8 0.0 copy-start.2
  55.8 0.7 copy-done.2
  56.5 0.0 copy-start.4
  56.5 0.6 copy-done.4
  57.1 0.0 copy-start.5
  57.1 0.6 copy-done.5
  57.7 0.0 copy-done.3
  57.7 0.0 copy-start.1
  57.7 0.0 copy-start.6
  57.7 111.2 %shard_map.138 = (f32[512,512]{1,0:T(8,128)}, f32[32,512]{1,0:T(8,128)}, f32[32,512]{1,0:T(8,128)}, f32[1,512]{1,0:T(1,128)}) custom-call(s32[1]{0:T(128)S(6)} %copy.19.task_ref, bf16[512,256]{1,0:T(8,128)(2,1)} %copy-done.2, s32[16,1,256]{2,1,0:T(1,128)} %copy-done.5, s32[64,1,128]{2,1,0:T(1,128)} %copy-done.4, s32[8,1,256]{2,1,0:T(1,128)} %copy-done.3, ...), custom_call_target="tpu_custom_call" | custom-call | tf_op jit(solution)/shard_map/pallas_call | solution.py:479
  168.9 0.0 copy-done.1
  168.9 0.0 copy-done.6
  168.9 0.0 copy-start.8
  168.9 0.0 copy-start.7
  168.9 0.0 copy-start.9
  168.9 2.9 %multiply_subtract_fusion = (f32[512,512]{1,0:T(8,128)}, f32[512,512]{1,0:T(8,128)}) fusion(f32[512,512]{1,0:T(8,128)} %get-tuple-element.15, f32[8,512,64]{1,2,0:T(8,128)S(1)} %copy-done.1, f32[8,512,64]{1,2,0:T(8,128)S(1)} %copy-done.6), kind=kLoop, calls=%fused_computation.1 | loop fusion | flops 1310720 | bytes 5242880 | tf_op jit(solution)/shard_map/sub | solution.py:541
  171.8 0.0 copy-done.8
  171.8 0.6 copy.20
  172.4 0.0 copy-done.7
  172.4 0.6 copy.21
  173.1 0.0 copy-done.9
  173.1 0.6 copy.22
Async XLA Ops:
  2.0 55.7 %copy-start.3 = (s32[8,1,256]{2,1,0:T(1,128)}, s32[8,1,256]{2,1,0:T(1,128)S(1)}, u32[]{:S(2)}) copy-start(s32[8,1,256]{2,1,0:T(1,128)S(1)} %reshape.36.bag_ref) | copy-start | bytes 24580
  4.3 1.2 copy-start
  55.8 0.7 copy-start.2
  56.5 0.6 copy-start.4
  57.1 0.6 copy-start.5
  57.7 111.2 %copy-start.1 = (f32[8,512,64]{1,2,0:T(8,128)S(1)}, f32[8,512,64]{1,2,0:T(8,128)}, u32[]{:S(2)}) copy-start(f32[8,512,64]{1,2,0:T(8,128)} %param.10) | copy-start | bytes 3145732
  57.7 111.2 %copy-start.6 = (f32[8,512,64]{1,2,0:T(8,128)S(1)}, f32[8,512,64]{1,2,0:T(8,128)}, u32[]{:S(2)}) copy-start(f32[8,512,64]{1,2,0:T(8,128)} %param.11) | copy-start | bytes 3145732
  168.9 2.9 %copy-start.8 = (f32[32,512]{1,0:T(8,128)S(1)}, f32[32,512]{1,0:T(8,128)}, u32[]{:S(2)}) copy-start(f32[32,512]{1,0:T(8,128)} %get-tuple-element.28) | copy-start | bytes 196612
  168.9 3.5 %copy-start.7 = (f32[32,512]{1,0:T(8,128)S(1)}, f32[32,512]{1,0:T(8,128)}, u32[]{:S(2)}) copy-start(f32[32,512]{1,0:T(8,128)} %get-tuple-element.29) | copy-start | bytes 196612
  168.9 4.2 %copy-start.9 = (f32[1,512]{1,0:T(1,128)S(1)}, f32[1,512]{1,0:T(1,128)}, u32[]{:S(2)}) copy-start(f32[1,512]{1,0:T(1,128)} %get-tuple-element.30) | copy-start | bytes 6148

commit v2 on v1

v2 whole, which is shorter than its diff:
```python
import jax
import jax.numpy as jnp
from jax import lax
from jax.experimental import pallas as pl
from jax.experimental.pallas import tpu as pltpu
from jax.sharding import PartitionSpec as P

MESH = pl.DeviceIdType.MESH
learn_rate = 0.2
f32 = jnp.float32
bf16 = jnp.bfloat16
i32 = jnp.int32

EMB = 64
SEC = 4
XS = 4
ZS = 8
CAP = 128
DIM = 64
SLOTS = 8
BATCH = 256
ROWS = 512
WIDE = 512


def mm(a, b):
    return lax.dot_general(a, b, (((1,), (0,)), ((), ())), preferred_element_type=f32)


def mm_nt(a, b):
    return lax.dot_general(a, b, (((1,), (1,)), ((), ())), preferred_element_type=f32)


def silu_slope(value):
    logistic = jax.nn.sigmoid(value)
    return logistic * (1.0 + value * (1.0 - logistic))


def hot(size, keys):
    rows = lax.broadcasted_iota(i32, (size, keys.shape[1]), 0)
    return jnp.where(rows == keys, 1.0, 0.0).astype(bf16)


SKIP = ()


class Nothing:
    def start(self):
        pass

    wait = wait_send = wait_recv = start


def remote(src, dst, send, recv, tag, **where):
    if tag in SKIP:
        return Nothing()
    return pltpu.make_async_remote_copy(
        src_ref=src, dst_ref=dst, send_sem=send, recv_sem=recv, device_id=where, device_id_type=MESH
    )


def greet(emb, sec):
    barrier = pltpu.get_barrier_semaphore()

    @pl.loop(1, EMB)
    def _(d):
        pl.semaphore_signal(barrier, inc=1, device_id={"emb": lax.rem(emb + d, EMB)}, device_id_type=MESH)

    for d in range(1, SEC):
        pl.semaphore_signal(barrier, inc=1, device_id={"sec": lax.rem(sec + d, SEC)}, device_id_type=MESH)


def meet():
    pl.semaphore_wait(pltpu.get_barrier_semaphore(), EMB - 1 + SEC - 1)


def route(ids_ref, ob, pos):
    before = lax.broadcasted_iota(i32, (BATCH, BATCH), 0)
    after = lax.broadcasted_iota(i32, (BATCH, BATCH), 1)
    upper = jnp.where(before < after, 1.0, 0.0).astype(bf16)
    shard_row = lax.broadcasted_iota(i32, (EMB, BATCH), 0)
    rank_row = lax.broadcasted_iota(i32, (CAP, BATCH), 0)
    carry = jnp.zeros((EMB, 1), f32)
    total = jnp.zeros((EMB, 2 * CAP), f32)
    for q in range(2 * SLOTS):
        ids = ids_ref[q // 2, q % 2 : q % 2 + 1, :]
        owner = ids >> 9
        key = (ids & (ROWS - 1)) + ((q // 2) * ROWS + 1)
        owned = jnp.where(shard_row == owner, 1.0, 0.0)
        owned_b = owned.astype(bf16)
        prefix = mm(owned_b, upper) + carry
        rank = jnp.sum(owned * prefix, axis=0, keepdims=True).astype(i32)
        carry = carry + jnp.sum(owned, axis=1, keepdims=True)
        pos[q] = owner * CAP + rank
        ranked = rank_row == rank
        high = jnp.where(ranked, (key >> 6).astype(f32), 0.0).astype(bf16)
        low = jnp.where(ranked, (key & 63).astype(f32), 0.0).astype(bf16)
        total = total + mm_nt(owned_b, jnp.concatenate([high, low], axis=0))
    keys = (total[:, :CAP] * 64.0 + total[:, CAP:]).astype(i32) - 1
    for s in range(EMB):
        ob[s] = keys[s : s + 1, :]


def step_kernel(
    task_ref, ids_ref, bag_ref, table_ref, expert_hbm, tower_hbm, out_row_ref, click_ref, watch_ref,
    grad_ref, packed_ref,
    pos, ob, ib, out_rows, in_rows, wide_rows, pooled_ref, tb, expert_ref, tower_ref,
    feats, hiddens, expert_t, tower_t, pre_e, pre_t, shares, part_out, part_in, whole, own_part,
    core_out, core_in, x_out, x_in, z_out, z_in, head_core, head_x, head_z,
    spread, out_grads, in_grads,
    load_sem, id_send, id_recv, row_send, row_recv,
    feat_sem, hidden_sem, share_sem, part_sem, core_sem, x_sem, z_sem, hcore_sem, hx_sem, hz_sem, grad_send, grad_recv,
):
    me = lax.axis_index("emb")
    sec = lax.axis_index("sec")
    core = lax.rem(me, 2)
    z = lax.rem(lax.div(me, 2), ZS)
    x = lax.div(me, 2 * ZS)
    half = lax.div(me, 32)
    inner = lax.rem(me, 32)
    partner = me + 1 - 2 * core
    expert_load = pltpu.make_async_copy(expert_hbm, expert_ref, load_sem.at[0])
    tower_load = pltpu.make_async_copy(tower_hbm, tower_ref, load_sem.at[1])
    expert_load.start()
    tower_load.start()
    greet(me, sec)
    route(ids_ref, ob, pos)
    meet()

    def rows_of(r):
        return pl.ds(pl.multiple_of(r * WIDE, WIDE), WIDE)

    def ahead(d):
        group = lax.rem(half + lax.div(d, 32), 2)
        return group * 32 + lax.rem(inner + d, 32)

    def behind(d):
        group = lax.rem(half + lax.div(d, 32), 2)
        return group * 32 + lax.rem(inner + 64 - d, 32)

    def id_copy(peer, at):
        return remote(ob.at[peer], ib.at[at], id_send.at[peer], id_recv.at[at], tag="ids", emb=peer)

    def row_copy(peer, at):
        return remote(out_rows.at[peer], in_rows.at[at], row_send.at[peer], row_recv.at[at], tag="rows", emb=peer)

    def grad_copy(peer, at):
        return remote(out_grads.at[peer], in_grads.at[at], grad_send.at[peer], grad_recv.at[at], tag="grads", emb=peer)

    @pl.loop(1, EMB)
    def _(d):
        id_copy(ahead(d), me).start()

    ib[me] = ob[me]
    tb[...] = table_ref[...].astype(bf16)
    expert_load.wait()
    tower_load.wait()

    if "transpose" not in SKIP:

        @pl.loop(0, SEC)
        def _(r):
            expert_t[r] = expert_ref[rows_of(r), :].T
            tower_t[r] = tower_ref[rows_of(r), :].T

    @pl.loop(0, EMB // 2)
    def _(t):
        a = behind(2 * t)
        b = behind(2 * t + 1)

        @pl.when(t > 0)
        def _():
            id_copy(a, a).wait_recv()

        id_copy(b, b).wait_recv()
        if "gather" not in SKIP:
            keys = jnp.concatenate([ib[a], ib[b]], axis=1)
            slot = keys >> 9
            picked = mm(tb[...], hot(ROWS, keys & (ROWS - 1)))
            rows = jnp.zeros((DIM, 2 * CAP), f32)
            for s in range(SLOTS):
                rows = rows + jnp.where(slot == s, picked[s * DIM : (s + 1) * DIM], 0.0)
            rows = rows.astype(bf16)
            out_rows[a] = rows[:, :CAP]
            out_rows[b] = rows[:, CAP:]

            @pl.when(t == 0)
            def _():
                in_rows[me] = rows[:, :CAP]

        @pl.when(t > 0)
        def _():
            row_copy(a, me).start()

        row_copy(b, me).start()

    def pool(part, first):
        for h in range(4):
            wide_rows[:, h * CAP : (h + 1) * CAP] = in_rows[pl.ds((part * 4 + h) * 8, 8)].reshape(8 * DIM, CAP)

        @pl.loop(0, SLOTS)
        def _(s):
            rows = pl.ds(pl.multiple_of(s * DIM, DIM), DIM)
            pooled = jnp.zeros((DIM, BATCH), f32) if first else pooled_ref[rows, :]
            for k in range(2):
                place = pos[2 * s + k]
                shard = place >> 7
                low = jnp.where(bag_ref[pl.ds(s, 1), :] > k, shard & 7, -1)
                key = ((shard >> 3) - part * 4) * CAP + (place & (CAP - 1))
                picked = mm(wide_rows[...], hot(4 * CAP, key))
                for g in range(8):
                    pooled = pooled + jnp.where(low == g, picked[g * DIM : (g + 1) * DIM], 0.0)
            if first:
                pooled_ref[rows, :] = pooled
            else:
                feats[sec, rows, :] = pooled.astype(bf16)

    @pl.loop(1, 32)
    def _(d):
        peer = ahead(d)
        row_copy(peer, peer).wait_recv()

    if "pool" not in SKIP:
        pool(half, True)

    @pl.loop(32, EMB)
    def _(d):
        peer = ahead(d)
        row_copy(peer, peer).wait_recv()

    if "pool" not in SKIP:
        pool(1 - half, False)

    def across(d):
        return lax.rem(sec + d, SEC)

    def sec_copy(buffer, sems, tag, d, at):
        return remote(buffer.at[sec], buffer.at[at], sems.at[0, d], sems.at[1, at], tag=tag, sec=across(d))

    def spread_out(buffer, sems, tag):
        for d in (2, 1, 3):
            sec_copy(buffer, sems, tag, d, sec).start()

    def arrive(buffer, sems, tag, d):
        sec_copy(buffer, sems, tag, d, across(d)).wait_recv()

    def left(buffer, sems, tag):
        for d in (2, 1, 3):
            sec_copy(buffer, sems, tag, d, sec).wait_send()

    spread_out(feats, feat_sem, "feats")
    pre_e[...] = mm(expert_t[sec], feats[sec])
    for d in (1, 3, 2):
        arrive(feats, feat_sem, "feats", d)
        pre_e[...] += mm(expert_t[across(d)], feats[across(d)])
    hiddens[sec] = jax.nn.silu(pre_e[...]).astype(bf16)
    spread_out(hiddens, hidden_sem, "hiddens")
    pre_t[...] = mm(tower_t[sec], hiddens[sec])
    for d in (1, 3, 2):
        arrive(hiddens, hidden_sem, "hiddens", d)
        pre_t[...] += mm(tower_t[across(d)], hiddens[across(d)])
    out_col = jnp.broadcast_to(out_row_ref[...], (8, WIDE)).T[:, 0:1]
    active = jax.nn.silu(pre_t[...])
    share = jnp.sum(active * out_col, axis=0, keepdims=True)
    chosen = jnp.where(lax.broadcasted_iota(i32, (8, BATCH), 0) == task_ref[0], 1.0, 0.0)
    shares[sec] = share * chosen
    spread_out(shares, share_sem, "shares")
    slope = out_col * silu_slope(pre_t[...])
    for d in (1, 3, 2):
        arrive(shares, share_sem, "shares", d)
    logits = (shares[0] + shares[1]) + (shares[2] + shares[3])
    err = logits[0:1] + logits[1:2] + logits[2:3] - watch_ref[...]
    chance = jax.nn.sigmoid(logits[0:2]) - click_ref[...] + err
    back = chance[0:1] * chosen[0:1] + chance[1:2] * chosen[1:2] + err * chosen[2:3]
    tower_delta = (back * slope).astype(bf16)

    def part_copy(n, d, at):
        return remote(part_out.at[n, d], part_in.at[n, at], part_sem.at[n, 0, d], part_sem.at[n, 1, at], tag="part", sec=across(d))

    def part(n, weights_ref, delta):
        for d in (2, 1, 3):
            peer = across(d)
            part_out[n, d] = mm(weights_ref[rows_of(peer), :], delta).astype(bf16)
            part_copy(n, d, sec).start()
        own_part[...] = mm(weights_ref[rows_of(sec), :], delta)

    def part_sum(n):
        for d in (1, 3, 2):
            part_copy(n, d, across(d)).wait_recv()
            own_part[...] += part_in[n, across(d)].astype(f32)
        for d in (2, 1, 3):
            part_copy(n, d, sec).wait_send()

    def core_copy(n):
        return remote(core_out.at[n], core_in.at[n], core_sem.at[0, n], core_sem.at[1, n], tag="core", emb=partner)

    def weight_grad(n, source, delta):
        @pl.loop(0, SEC)
        def _(r):
            whole[n, pl.ds(r * 16, 16)] = mm_nt(source[r], delta).reshape(16, 32, WIDE)

        @pl.loop(0, 32)
        def _(j):
            core_out[n, j] = whole[n, 2 * j + 1 - core].astype(bf16)

        core_copy(n).start()

    def x_copy(n, d):
        to = lax.rem(x + d, XS)
        return remote(
            x_out.at[n, to], x_in.at[n, x], x_sem.at[n, 0, d], x_sem.at[n, 1, x], tag="x", emb=(to * ZS + z) * 2 + core
        )

    def x_arrive(n, d):
        to = lax.rem(x + d, XS)
        return remote(
            x_out.at[n, to], x_in.at[n, to], x_sem.at[n, 0, d], x_sem.at[n, 1, to], tag="x", emb=(to * ZS + z) * 2 + core
        )

    def z_copy(n, d):
        to = lax.rem(z + d, ZS)
        return remote(
            z_out.at[n, to], z_in.at[n, z], z_sem.at[n, 0, d], z_sem.at[n, 1, z], tag="z", emb=(x * ZS + to) * 2 + core
        )

    def z_arrive(n, d):
        to = lax.rem(z + d, ZS)
        return remote(
            z_out.at[n, to], z_in.at[n, to], z_sem.at[n, 0, d], z_sem.at[n, 1, to], tag="z", emb=(x * ZS + to) * 2 + core
        )

    def core_sum(n):
        core_copy(n).wait()

        @pl.loop(0, 32)
        def _(j):
            value = whole[n, 2 * j + core] + core_in[n, j].astype(f32)
            whole[n, 2 * j + core] = value
            x_out[n, lax.div(j, ZS), lax.rem(j, ZS)] = value.astype(bf16)

        for d in (2, 1, 3):
            x_copy(n, d).start()

    def x_sum(n):
        for d in (1, 3, 2):
            x_arrive(n, d).wait_recv()

        @pl.loop(0, ZS)
        def _(j):
            at = 2 * (x * ZS + j) + core
            value = whole[n, at]
            for d in range(1, XS):
                value = value + x_in[n, lax.rem(x + d, XS), j].astype(f32)
            whole[n, at] = value
            z_out[n, j] = value.astype(bf16)

        for d in range(1, ZS):
            z_copy(n, d).start()

    def z_sum(n):
        for d in range(1, ZS):
            z_arrive(n, d).wait_recv()
        value = whole[n, me]
        for d in range(1, ZS):
            value = value + z_in[n, lax.rem(z + d, ZS)].astype(f32)
        packed_ref[pl.ds(32 * n, 32), :] = value
        for d in range(1, XS):
            x_copy(n, d).wait_send()
        for d in range(1, ZS):
            z_copy(n, d).wait_send()

    def hc_copy():
        return remote(head_core.at[0], head_core.at[1], hcore_sem.at[0], hcore_sem.at[1], tag="head", emb=partner)

    def hx_copy(d, at):
        to = lax.rem(x + d, XS)
        return remote(head_x.at[x], head_x.at[at], hx_sem.at[0, d], hx_sem.at[1, at], tag="head", emb=(to * ZS + z) * 2 + core)

    def hz_copy(d, at):
        to = lax.rem(z + d, ZS)
        return remote(head_z.at[z], head_z.at[at], hz_sem.at[0, d], hz_sem.at[1, at], tag="head", emb=(x * ZS + to) * 2 + core)

    part(0, tower_ref, tower_delta)
    head_core[0] = lax.dot_general(
        back, active, (((1,), (1,)), ((), ())), preferred_element_type=f32, precision=lax.Precision.HIGHEST
    )
    hc_copy().start()
    weight_grad(0, hiddens, tower_delta)
    hc_copy().wait()
    head_x[x] = head_core[0] + head_core[1]
    for d in range(1, XS):
        hx_copy(d, x).start()
    core_sum(0)
    left(feats, feat_sem, "feats")
    left(hiddens, hidden_sem, "hiddens")
    left(shares, share_sem, "shares")
    for d in range(1, XS):
        hx_copy(d, lax.rem(x + d, XS)).wait_recv()
    head_z[z] = (head_x[0] + head_x[1]) + (head_x[2] + head_x[3])
    for d in range(1, ZS):
        hz_copy(d, z).start()

    part_sum(0)
    expert_delta = (own_part[...] * silu_slope(pre_e[...])).astype(bf16)
    part(1, expert_ref, expert_delta)
    weight_grad(1, feats, expert_delta)
    x_sum(0)
    core_sum(1)
    part_sum(1)

    @pl.loop(0, SLOTS)
    def _(s):
        grad = own_part[pl.ds(pl.multiple_of(s * DIM, DIM), DIM), :]
        for k in range(2):
            low = jnp.where(bag_ref[pl.ds(s, 1), :] > k, (pos[2 * s + k] >> 7) & 7, -1)
            for g in range(8):
                spread[2 * s + k, g * DIM : (g + 1) * DIM, :] = jnp.where(low == g, grad, 0.0).astype(bf16)

    @pl.loop(0, 4)
    def _(t):
        pair = lax.rem(x + t, 4)

        def add(q, total):
            place = pos[q]
            key = ((place >> 10) - 2 * pair) * CAP + (place & (CAP - 1))
            return total + mm_nt(spread[q], hot(2 * CAP, key))

        total = lax.fori_loop(0, 2 * SLOTS, add, jnp.zeros((8 * DIM, 2 * CAP), f32)).astype(bf16)
        for h in range(2):
            for g in range(8):
                peer = (2 * pair + h) * 8 + g
                out_grads[peer] = total[g * DIM : (g + 1) * DIM, h * CAP : (h + 1) * CAP]

                @pl.when(peer != me)
                def _():
                    grad_copy(peer, me).start()

                @pl.when(peer == me)
                def _():
                    in_grads[me] = total[g * DIM : (g + 1) * DIM, h * CAP : (h + 1) * CAP]

    x_sum(1)
    z_sum(0)
    for d in range(1, ZS):
        hz_copy(d, lax.rem(z + d, ZS)).wait_recv()
    head = head_z[0]
    for j in range(1, ZS):
        head = head + head_z[j]
    packed_ref[64:72, :] = jnp.broadcast_to(head, (8, WIDE))

    grad_ref[...] = jnp.zeros((WIDE, ROWS), f32)

    @pl.loop(0, XS)
    def _(t):
        first = lax.rem(x + XS - t, XS) * 16

        @pl.loop(0, 16)
        def _(j):
            peer = first + j

            @pl.when(peer != me)
            def _():
                grad_copy(peer, peer).wait_recv()

        if "scatter" not in SKIP:

            @pl.loop(0, 8)
            def _(j):
                a = first + 2 * j
                keys = jnp.concatenate([ib[a], ib[a + 1]], axis=1)
                slot = keys >> 9
                grads = jnp.concatenate([in_grads[a], in_grads[a + 1]], axis=1).astype(f32)
                wide = jnp.concatenate([jnp.where(slot == s, grads, 0.0) for s in range(SLOTS)], axis=0).astype(bf16)
                grad_ref[...] += mm_nt(wide, hot(ROWS, keys & (ROWS - 1)))

    z_sum(1)
    for d in range(1, XS):
        hx_copy(d, x).wait_send()
    for d in range(1, ZS):
        hz_copy(d, z).wait_send()

    @pl.loop(1, EMB)
    def _(d):
        peer = lax.rem(me + d, EMB)
        id_copy(peer, me).wait_send()
        row_copy(peer, me).wait_send()
        grad_copy(peer, me).wait_send()


def body(
    emb_table,
    emb_accum,
    slot_ids,
    bag_len,
    expert_w,
    tower_w,
    tower_out,
    section_task,
    click_like,
    watch,
):
    vmem = pl.BlockSpec(memory_space=pltpu.VMEM)
    dma = pltpu.SemaphoreType.DMA
    table = emb_table.transpose(0, 2, 1).reshape(SLOTS * DIM, ROWS)
    accum = emb_accum.transpose(0, 2, 1).reshape(SLOTS * DIM, ROWS)
    anywhere = pl.BlockSpec(memory_space=pl.ANY)
    row_grad, packed = pl.pallas_call(
        step_kernel,
        out_shape=(
            jax.ShapeDtypeStruct((SLOTS * DIM, ROWS), f32),
            jax.ShapeDtypeStruct((72, WIDE), f32),
        ),
        in_specs=[pl.BlockSpec(memory_space=pltpu.SMEM), vmem, vmem, vmem, anywhere, anywhere, vmem, vmem, vmem],
        out_specs=(vmem,) * 2,
        scratch_shapes=[
            pltpu.VMEM((2 * SLOTS, 1, BATCH), i32),
            pltpu.VMEM((EMB, 1, CAP), i32),
            pltpu.VMEM((EMB, 1, CAP), i32),
            pltpu.VMEM((EMB, DIM, CAP), bf16),
            pltpu.VMEM((EMB, DIM, CAP), bf16),
            pltpu.VMEM((8 * DIM, 4 * CAP), bf16),
            pltpu.VMEM((8 * DIM, BATCH), f32),
            pltpu.VMEM((SLOTS * DIM, ROWS), bf16),
            pltpu.VMEM((SEC * WIDE, WIDE), bf16),
            pltpu.VMEM((SEC * WIDE, WIDE), bf16),
            pltpu.VMEM((SEC, WIDE, BATCH), bf16),
            pltpu.VMEM((SEC, WIDE, BATCH), bf16),
            pltpu.VMEM((SEC, WIDE, WIDE), bf16),
            pltpu.VMEM((SEC, WIDE, WIDE), bf16),
            pltpu.VMEM((WIDE, BATCH), f32),
            pltpu.VMEM((WIDE, BATCH), f32),
            pltpu.VMEM((SEC, 8, BATCH), f32),
            pltpu.VMEM((2, SEC, WIDE, BATCH), bf16),
            pltpu.VMEM((2, SEC, WIDE, BATCH), bf16),
            pltpu.VMEM((2, EMB, 32, WIDE), f32),
            pltpu.VMEM((WIDE, BATCH), f32),
            pltpu.VMEM((2, 32, 32, WIDE), bf16),
            pltpu.VMEM((2, 32, 32, WIDE), bf16),
            pltpu.VMEM((2, XS, ZS, 32, WIDE), bf16),
            pltpu.VMEM((2, XS, ZS, 32, WIDE), bf16),
            pltpu.VMEM((2, ZS, 32, WIDE), bf16),
            pltpu.VMEM((2, ZS, 32, WIDE), bf16),
            pltpu.VMEM((2, 1, WIDE), f32),
            pltpu.VMEM((XS, 1, WIDE), f32),
            pltpu.VMEM((ZS, 1, WIDE), f32),
            pltpu.VMEM((2 * SLOTS, 8 * DIM, BATCH), bf16),
            pltpu.VMEM((EMB, DIM, CAP), bf16),
            pltpu.VMEM((EMB, DIM, CAP), bf16),
            dma((2,)),
            dma((EMB,)),
            dma((EMB,)),
            dma((EMB,)),
            dma((EMB,)),
            dma((2, SEC)),
            dma((2, SEC)),
            dma((2, SEC)),
            dma((2, 2, SEC)),
            dma((2, 2)),
            dma((2, 2, XS)),
            dma((2, 2, ZS)),
            dma((2,)),
            dma((2, XS)),
            dma((2, ZS)),
            dma((EMB,)),
            dma((EMB,)),
        ],
        compiler_params=pltpu.CompilerParams(collective_id=0, has_side_effects=True, vmem_limit_bytes=60 << 20),
    )(
        section_task,
        slot_ids.transpose(1, 2, 0),
        bag_len.T,
        table,
        expert_w,
        tower_w,
        tower_out,
        click_like.T,
        watch.reshape(1, BATCH),
    )
    tower_grad, expert_grad, head_grad = packed[:32], packed[32:64], packed[64:65]
    new_accum = accum + row_grad * row_grad
    new_table = table - learn_rate * row_grad / jnp.sqrt(new_accum)

    def back(value):
        return value.reshape(SLOTS, DIM, ROWS).transpose(0, 2, 1)

    return (back(new_table), back(new_accum), expert_grad, tower_grad, head_grad)


def solution(mesh):
    placed = (
        P("sec", "emb", None),
        P("sec", "emb", None),
        P("emb", "sec", None),
        P("emb", "sec"),
        P(None, "sec"),
        P(None, "sec"),
        P("sec", None),
        P("sec"),
        P("emb", None),
        P("emb"),
    )
    return jax.shard_map(
        body,
        mesh=mesh,
        in_specs=placed,
        out_specs=(
            P("sec", "emb", None),
            P("sec", "emb", None),
            P("emb", "sec"),
            P("emb", "sec"),
            P("sec", None),
        ),
        check_vma=False,
    )
```

time: 174 us -> 159 us (0.914)
  Pallas kernels: 161 us -> 152 us
  local copies, waits for them, and re-layouts: 7.98 us -> 2.83 us
    pallas_call x1 -> x0, Pallas kernels: 50.3 us -> none  [body(): pl.pallas_call(lookup_kernel, out_shape=(jax.ShapeDtypeStruct((SLOTS * DI...]
    pallas_call x1, Pallas kernels: 111 us -> 152 us  [body(): pl.pallas_call(step_kernel, out_shape=(jax.ShapeDtypeStruct((SLOTS * DIM,...]
    unnamed x23 -> x4, local copies, waits for them, and re-layouts: 5 us -> 0.01 us
    reshape x3 -> x0, local copies, waits for them, and re-layouts: 2.98 us -> none  [the longest x1 1.54 us: body(): tower_out.reshape(WIDE, 1)]
    slice x0 -> x2, local copies, waits for them, and re-layouts: none -> 2.82 us  [the longest x1 1.53 us: body(): packed[:32]]
where the time goes in v2:
time: 159 us
  Pallas kernels  152 us (96%)
  other arithmetic  2.85 us (2%)
  local copies, waits for them, and re-layouts  2.83 us (2%)
    pallas_call x1, Pallas kernels, body(): pl.pallas_call(step_kernel, out_shape=(jax.ShapeDtypeStruct((SLOTS * DIM,...  152 us

profile of v2, /device:TPU:1, one launch (start us, length us, event | category | flops | bytes accessed | tf_op | source)
XLA Modules:
  0.0 159.0 jit_solution(12829132851193990942)
XLA Ops:
  1.3 0.0 copy-start
  1.3 0.0 copy-start.1
  1.3 152.0 %shard_map.137 = (f32[512,512]{1,0:T(8,128)}, f32[72,512]{1,0:T(8,128)}) custom-call(s32[1]{0:T(128)S(6)} %copy.15.task_ref, s32[8,2,256]{2,1,0:T(2,128)} %bitcast.22, s32[8,256]{1,0:T(8,128)} %bitcast.23, f32[512,512]{1,0:T(8,128)} %bitcast.19, bf16[2048,512]{1,0:T(8,128)(2,1)} %expert_hbm.1, bf16[2048,512]{1,0:T(8,128)(2,1)} %tower_hbm.1, ...), custom_call_target="tpu_custom_call" | custom-call | tf_op jit(solution)/shard_map/pallas_call | solution.py:507
  153.3 1.3 slice.11
  154.6 1.5 fusion
  156.2 0.0 copy-done
  156.2 0.0 copy-done.1
  156.2 2.8 %multiply_subtract_fusion = (f32[512,512]{1,0:T(8,128)}, f32[512,512]{1,0:T(8,128)}) fusion(f32[512,512]{1,0:T(8,128)} %get-tuple-element.7, f32[8,512,64]{1,2,0:T(8,128)S(1)} %copy-done, f32[8,512,64]{1,2,0:T(8,128)S(1)} %copy-done.1), kind=kLoop, calls=%fused_computation.1 | loop fusion | flops 1310720 | bytes 5242880 | tf_op jit(solution)/shard_map/sub | solution.py:581
Async XLA Ops:
  1.3 154.9 %copy-start = (f32[8,512,64]{1,2,0:T(8,128)S(1)}, f32[8,512,64]{1,2,0:T(8,128)}, u32[]{:S(2)}) copy-start(f32[8,512,64]{1,2,0:T(8,128)} %param.10) | copy-start | bytes 3145732
  1.3 154.9 %copy-start.1 = (f32[8,512,64]{1,2,0:T(8,128)S(1)}, f32[8,512,64]{1,2,0:T(8,128)}, u32[]{:S(2)}) copy-start(f32[8,512,64]{1,2,0:T(8,128)} %param.11) | copy-start | bytes 3145732

commit v3 on v2

--- a/solution.py
+++ b/solution.py
@@ -105,9 +105,9 @@
     task_ref, ids_ref, bag_ref, table_ref, expert_hbm, tower_hbm, out_row_ref, click_ref, watch_ref,
     grad_ref, packed_ref,
     pos, ob, ib, out_rows, in_rows, wide_rows, pooled_ref, tb, expert_ref, tower_ref,
-    feats, hiddens, expert_t, tower_t, pre_e, pre_t, shares, part_out, part_in, whole, own_part,
+    feats, hiddens, expert_t, tower_t, pre_e, pre_t, shares, part_out, part_in, relay, whole, own_part,
     core_out, core_in, x_out, x_in, z_out, z_in, head_core, head_x, head_z,
-    spread, out_grads, in_grads,
+    spread, hots, row_hots, out_grads, in_grads,
     load_sem, id_send, id_recv, row_send, row_recv,
     feat_sem, hidden_sem, share_sem, part_sem, core_sem, x_sem, z_sem, hcore_sem, hx_sem, hz_sem, grad_send, grad_recv,
 ):
@@ -237,59 +237,94 @@
     def sec_copy(buffer, sems, tag, d, at):
         return remote(buffer.at[sec], buffer.at[at], sems.at[0, d], sems.at[1, at], tag=tag, sec=across(d))
 
-    def spread_out(buffer, sems, tag):
-        for d in (2, 1, 3):
-            sec_copy(buffer, sems, tag, d, sec).start()
-
-    def arrive(buffer, sems, tag, d):
-        sec_copy(buffer, sems, tag, d, across(d)).wait_recv()
+    def ring_copy(buffer, sems, tag, i, arriving=False):
+        offset, part, way = ((0, 0, 1), (0, 1, 1), (0, 1, 3), (0, 0, 3), (3, 0, 1), (1, 1, 3))[i]
+        rows = pl.ds(part * (WIDE // 2), WIDE // 2)
+        source = across(offset)
+        target = across(4 - way + offset) if arriving else source
+        return remote(
+            buffer.at[source, rows], buffer.at[target, rows], sems.at[0, i], sems.at[1, i], tag=tag, sec=across(way)
+        )
+
+    def gather_sec(buffer, sems, tag, weights, total):
+        def came(i):
+            ring_copy(buffer, sems, tag, i, True).wait_recv()
+
+        total[...] = mm(weights[sec], buffer[sec])
+        came(0)
+        ring_copy(buffer, sems, tag, 4).start()
+        came(2)
+        ring_copy(buffer, sems, tag, 5).start()
+        came(1)
+        total[...] += mm(weights[across(3)], buffer[across(3)])
+        came(3)
+        total[...] += mm(weights[across(1)], buffer[across(1)])
+        came(4)
+        came(5)
+        total[...] += mm(weights[across(2)], buffer[across(2)])
 
     def left(buffer, sems, tag):
-        for d in (2, 1, 3):
-            sec_copy(buffer, sems, tag, d, sec).wait_send()
-
-    spread_out(feats, feat_sem, "feats")
-    pre_e[...] = mm(expert_t[sec], feats[sec])
-    for d in (1, 3, 2):
-        arrive(feats, feat_sem, "feats", d)
-        pre_e[...] += mm(expert_t[across(d)], feats[across(d)])
+        for i in range(6):
+            ring_copy(buffer, sems, tag, i).wait_send()
+
+    for i in (0, 2, 1, 3):
+        ring_copy(feats, feat_sem, "feats", i).start()
+    gather_sec(feats, feat_sem, "feats", expert_t, pre_e)
     hiddens[sec] = jax.nn.silu(pre_e[...]).astype(bf16)
-    spread_out(hiddens, hidden_sem, "hiddens")
-    pre_t[...] = mm(tower_t[sec], hiddens[sec])
-    for d in (1, 3, 2):
-        arrive(hiddens, hidden_sem, "hiddens", d)
-        pre_t[...] += mm(tower_t[across(d)], hiddens[across(d)])
+    for i in (0, 2, 1, 3):
+        ring_copy(hiddens, hidden_sem, "hiddens", i).start()
+    gather_sec(hiddens, hidden_sem, "hiddens", tower_t, pre_t)
     out_col = jnp.broadcast_to(out_row_ref[...], (8, WIDE)).T[:, 0:1]
     active = jax.nn.silu(pre_t[...])
     share = jnp.sum(active * out_col, axis=0, keepdims=True)
     chosen = jnp.where(lax.broadcasted_iota(i32, (8, BATCH), 0) == task_ref[0], 1.0, 0.0)
     shares[sec] = share * chosen
-    spread_out(shares, share_sem, "shares")
+    for d in (2, 1, 3):
+        sec_copy(shares, share_sem, "shares", d, sec).start()
     slope = out_col * silu_slope(pre_t[...])
     for d in (1, 3, 2):
-        arrive(shares, share_sem, "shares", d)
+        sec_copy(shares, share_sem, "shares", d, across(d)).wait_recv()
     logits = (shares[0] + shares[1]) + (shares[2] + shares[3])
     err = logits[0:1] + logits[1:2] + logits[2:3] - watch_ref[...]
     chance = jax.nn.sigmoid(logits[0:2]) - click_ref[...] + err
     back = chance[0:1] * chosen[0:1] + chance[1:2] * chosen[1:2] + err * chosen[2:3]
     tower_delta = (back * slope).astype(bf16)
 
-    def part_copy(n, d, at):
-        return remote(part_out.at[n, d], part_in.at[n, at], part_sem.at[n, 0, d], part_sem.at[n, 1, at], tag="part", sec=across(d))
+    low_half = slice(0, WIDE // 2)
+    high_half = slice(WIDE // 2, WIDE)
+
+    def part_copy(n, i):
+        return remote(
+            part_out.at[n, i], part_in.at[n, i], part_sem.at[n, 0, i], part_sem.at[n, 1, i],
+            tag="part", sec=across((1, 3, 1, 3, 1, 3)[i]),
+        )
 
     def part(n, weights_ref, delta):
-        for d in (2, 1, 3):
-            peer = across(d)
-            part_out[n, d] = mm(weights_ref[rows_of(peer), :], delta).astype(bf16)
-            part_copy(n, d, sec).start()
+        def send(i, value):
+            part_out[n, i] = value.astype(bf16)
+            part_copy(n, i).start()
+
+        value = mm(weights_ref[rows_of(across(2)), :], delta)
+        send(0, value[low_half])
+        send(1, value[high_half])
+        value = mm(weights_ref[rows_of(across(1)), :], delta)
+        send(2, value[high_half])
+        relay[0] = value[low_half]
+        value = mm(weights_ref[rows_of(across(3)), :], delta)
+        send(3, value[low_half])
+        relay[1] = value[high_half]
         own_part[...] = mm(weights_ref[rows_of(sec), :], delta)
+        for i in range(2):
+            part_copy(n, i).wait_recv()
+            send(4 + i, relay[i] + part_in[n, i].astype(f32))
 
     def part_sum(n):
-        for d in (1, 3, 2):
-            part_copy(n, d, across(d)).wait_recv()
-            own_part[...] += part_in[n, across(d)].astype(f32)
-        for d in (2, 1, 3):
-            part_copy(n, d, sec).wait_send()
+        for i in range(2, 6):
+            part_copy(n, i).wait_recv()
+        own_part[low_half, :] += part_in[n, 3].astype(f32) + part_in[n, 4].astype(f32)
+        own_part[high_half, :] += part_in[n, 2].astype(f32) + part_in[n, 5].astype(f32)
+        for i in range(6):
+            part_copy(n, i).wait_send()
 
     def core_copy(n):
         return remote(core_out.at[n], core_in.at[n], core_sem.at[0, n], core_sem.at[1, n], tag="core", emb=partner)
@@ -393,7 +428,8 @@
     core_sum(0)
     left(feats, feat_sem, "feats")
     left(hiddens, hidden_sem, "hiddens")
-    left(shares, share_sem, "shares")
+    for d in (2, 1, 3):
+        sec_copy(shares, share_sem, "shares", d, sec).wait_send()
     for d in range(1, XS):
         hx_copy(d, lax.rem(x + d, XS)).wait_recv()
     head_z[z] = (head_x[0] + head_x[1]) + (head_x[2] + head_x[3])
@@ -413,19 +449,19 @@
         grad = own_part[pl.ds(pl.multiple_of(s * DIM, DIM), DIM), :]
         for k in range(2):
             low = jnp.where(bag_ref[pl.ds(s, 1), :] > k, (pos[2 * s + k] >> 7) & 7, -1)
+            columns = pl.ds(pl.multiple_of((2 * s + k) * BATCH, BATCH), BATCH)
             for g in range(8):
-                spread[2 * s + k, g * DIM : (g + 1) * DIM, :] = jnp.where(low == g, grad, 0.0).astype(bf16)
+                spread[g * DIM : (g + 1) * DIM, columns] = jnp.where(low == g, grad, 0.0).astype(bf16)
 
     @pl.loop(0, 4)
     def _(t):
         pair = lax.rem(x + t, 4)
 
-        def add(q, total):
+        for q in range(2 * SLOTS):
             place = pos[q]
             key = ((place >> 10) - 2 * pair) * CAP + (place & (CAP - 1))
-            return total + mm_nt(spread[q], hot(2 * CAP, key))
-
-        total = lax.fori_loop(0, 2 * SLOTS, add, jnp.zeros((8 * DIM, 2 * CAP), f32)).astype(bf16)
+            hots[:, q * BATCH : (q + 1) * BATCH] = hot(2 * CAP, key)
+        total = mm_nt(spread[...], hots[...]).astype(bf16)
         for h in range(2):
             for g in range(8):
                 peer = (2 * pair + h) * 8 + g
@@ -471,7 +507,11 @@
                 slot = keys >> 9
                 grads = jnp.concatenate([in_grads[a], in_grads[a + 1]], axis=1).astype(f32)
                 wide = jnp.concatenate([jnp.where(slot == s, grads, 0.0) for s in range(SLOTS)], axis=0).astype(bf16)
-                grad_ref[...] += mm_nt(wide, hot(ROWS, keys & (ROWS - 1)))
+                columns = pl.ds(pl.multiple_of(j * 2 * CAP, 2 * CAP), 2 * CAP)
+                spread[:, columns] = wide
+                row_hots[:, columns] = hot(ROWS, keys & (ROWS - 1))
+
+            grad_ref[...] += mm_nt(spread[:, : 16 * CAP], row_hots[...])
 
     z_sum(1)
     for d in range(1, XS):
@@ -530,8 +570,9 @@
             pltpu.VMEM((WIDE, BATCH), f32),
             pltpu.VMEM((WIDE, BATCH), f32),
             pltpu.VMEM((SEC, 8, BATCH), f32),
-            pltpu.VMEM((2, SEC, WIDE, BATCH), bf16),
-            pltpu.VMEM((2, SEC, WIDE, BATCH), bf16),
+            pltpu.VMEM((2, 6, WIDE // 2, BATCH), bf16),
+            pltpu.VMEM((2, 6, WIDE // 2, BATCH), bf16),
+            pltpu.VMEM((2, WIDE // 2, BATCH), f32),
             pltpu.VMEM((2, EMB, 32, WIDE), f32),
             pltpu.VMEM((WIDE, BATCH), f32),
             pltpu.VMEM((2, 32, 32, WIDE), bf16),
@@ -543,7 +584,9 @@
             pltpu.VMEM((2, 1, WIDE), f32),
             pltpu.VMEM((XS, 1, WIDE), f32),
             pltpu.VMEM((ZS, 1, WIDE), f32),
-            pltpu.VMEM((2 * SLOTS, 8 * DIM, BATCH), bf16),
+            pltpu.VMEM((8 * DIM, 2 * SLOTS * BATCH), bf16),
+            pltpu.VMEM((2 * CAP, 2 * SLOTS * BATCH), bf16),
+            pltpu.VMEM((ROWS, 16 * CAP), bf16),
             pltpu.VMEM((EMB, DIM, CAP), bf16),
             pltpu.VMEM((EMB, DIM, CAP), bf16),
             dma((2,)),
@@ -551,10 +594,10 @@
             dma((EMB,)),
             dma((EMB,)),
             dma((EMB,)),
+            dma((2, 6)),
+            dma((2, 6)),
             dma((2, SEC)),
-            dma((2, SEC)),
-            dma((2, SEC)),
-            dma((2, 2, SEC)),
+            dma((2, 2, 6)),
             dma((2, 2)),
             dma((2, 2, XS)),
             dma((2, 2, ZS)),

time: 159 us -> 149 us (0.937)
  Pallas kernels: 152 us -> 142 us
    pallas_call x1, Pallas kernels: 152 us -> 142 us  [body(): pl.pallas_call(step_kernel, out_shape=(jax.ShapeDtypeStruct((SLOTS * DIM,...]
where the time goes in v3:
time: 149 us
  Pallas kernels  142 us (95%)
  other arithmetic  2.85 us (2%)
  local copies, waits for them, and re-layouts  2.83 us (2%)
    pallas_call x1, Pallas kernels, body(): pl.pallas_call(step_kernel, out_shape=(jax.ShapeDtypeStruct((SLOTS * DIM,...  142 us

profile of v3, /device:TPU:1, one launch (start us, length us, event | category | flops | bytes accessed | tf_op | source)
XLA Modules:
  0.0 148.6 jit_solution(6911586277789637090)
XLA Ops:
  1.3 0.0 copy-start
  1.3 0.0 copy-start.1
  1.3 141.6 %shard_map.137 = (f32[512,512]{1,0:T(8,128)}, f32[72,512]{1,0:T(8,128)}) custom-call(s32[1]{0:T(128)S(6)} %copy.15.task_ref, s32[8,2,256]{2,1,0:T(2,128)} %bitcast.22, s32[8,256]{1,0:T(8,128)} %bitcast.23, f32[512,512]{1,0:T(8,128)} %bitcast.19, bf16[2048,512]{1,0:T(8,128)(2,1)} %expert_hbm.1, bf16[2048,512]{1,0:T(8,128)(2,1)} %tower_hbm.1, ...), custom_call_target="tpu_custom_call" | custom-call | tf_op jit(solution)/shard_map/pallas_call | solution.py:547
  142.9 1.3 slice.11
  144.2 1.5 %fusion = (f32[32,512]{1,0:T(8,128)}, f32[32,512]{1,0:T(8,128)}) fusion(f32[72,512]{1,0:T(8,128)} %get-tuple-element.8), kind=kLoop, calls=%fused_computation.2 | loop fusion | bytes 262144 | tf_op jit(solution)/shard_map/slice | solution.py:622
  145.7 0.0 copy-done
  145.7 0.0 copy-done.1
  145.7 2.8 %multiply_subtract_fusion = (f32[512,512]{1,0:T(8,128)}, f32[512,512]{1,0:T(8,128)}) fusion(f32[512,512]{1,0:T(8,128)} %get-tuple-element.7, f32[8,512,64]{1,2,0:T(8,128)S(1)} %copy-done, f32[8,512,64]{1,2,0:T(8,128)S(1)} %copy-done.1), kind=kLoop, calls=%fused_computation.1 | loop fusion | flops 1310720 | bytes 5242880 | tf_op jit(solution)/shard_map/sub | solution.py:624
Async XLA Ops:
  1.3 144.4 %copy-start = (f32[8,512,64]{1,2,0:T(8,128)S(1)}, f32[8,512,64]{1,2,0:T(8,128)}, u32[]{:S(2)}) copy-start(f32[8,512,64]{1,2,0:T(8,128)} %param.10) | copy-start | bytes 3145732
  1.3 144.4 %copy-start.1 = (f32[8,512,64]{1,2,0:T(8,128)S(1)}, f32[8,512,64]{1,2,0:T(8,128)}, u32[]{:S(2)}) copy-start(f32[8,512,64]{1,2,0:T(8,128)} %param.11) | copy-start | bytes 3145732

commit v4 on v3

--- a/solution.py
+++ b/solution.py
@@ -147,6 +147,42 @@
     def grad_copy(peer, at):
         return remote(out_grads.at[peer], in_grads.at[at], grad_send.at[peer], grad_recv.at[at], tag="grads", emb=peer)
 
+    def across(d):
+        return lax.rem(sec + d, SEC)
+
+    def sec_copy(buffer, sems, tag, d, at):
+        return remote(buffer.at[sec], buffer.at[at], sems.at[0, d], sems.at[1, at], tag=tag, sec=across(d))
+
+    def ring_copy(buffer, sems, tag, i, arriving=False):
+        offset, part, way = ((0, 0, 1), (0, 1, 1), (0, 1, 3), (0, 0, 3), (3, 0, 1), (1, 1, 3))[i]
+        rows = pl.ds(part * (WIDE // 2), WIDE // 2)
+        source = across(offset)
+        target = across(4 - way + offset) if arriving else source
+        return remote(
+            buffer.at[source, rows], buffer.at[target, rows], sems.at[0, i], sems.at[1, i], tag=tag, sec=across(way)
+        )
+
+    def gather_sec(buffer, sems, tag, weights, total):
+        def came(i):
+            ring_copy(buffer, sems, tag, i, True).wait_recv()
+
+        total[...] = mm(weights[sec], buffer[sec])
+        came(0)
+        ring_copy(buffer, sems, tag, 4).start()
+        came(2)
+        ring_copy(buffer, sems, tag, 5).start()
+        came(1)
+        total[...] += mm(weights[across(3)], buffer[across(3)])
+        came(3)
+        total[...] += mm(weights[across(1)], buffer[across(1)])
+        came(4)
+        came(5)
+        total[...] += mm(weights[across(2)], buffer[across(2)])
+
+    def left(buffer, sems, tag):
+        for i in range(6):
+            ring_copy(buffer, sems, tag, i).wait_send()
+
     @pl.loop(1, EMB)
     def _(d):
         id_copy(ahead(d), me).start()
@@ -194,11 +230,12 @@
 
         row_copy(b, me).start()
 
-    def pool(part, first):
+    def widen(part):
         for h in range(4):
             wide_rows[:, h * CAP : (h + 1) * CAP] = in_rows[pl.ds((part * 4 + h) * 8, 8)].reshape(8 * DIM, CAP)
 
-        @pl.loop(0, SLOTS)
+    def pool(part, first, begin, end):
+        @pl.loop(begin, end)
         def _(s):
             rows = pl.ds(pl.multiple_of(s * DIM, DIM), DIM)
             pooled = jnp.zeros((DIM, BATCH), f32) if first else pooled_ref[rows, :]
@@ -220,55 +257,21 @@
         peer = ahead(d)
         row_copy(peer, peer).wait_recv()
 
-    if "pool" not in SKIP:
-        pool(half, True)
+    widen(half)
+    pool(half, True, 0, SLOTS)
 
     @pl.loop(32, EMB)
     def _(d):
         peer = ahead(d)
         row_copy(peer, peer).wait_recv()
 
-    if "pool" not in SKIP:
-        pool(1 - half, False)
-
-    def across(d):
-        return lax.rem(sec + d, SEC)
-
-    def sec_copy(buffer, sems, tag, d, at):
-        return remote(buffer.at[sec], buffer.at[at], sems.at[0, d], sems.at[1, at], tag=tag, sec=across(d))
-
-    def ring_copy(buffer, sems, tag, i, arriving=False):
-        offset, part, way = ((0, 0, 1), (0, 1, 1), (0, 1, 3), (0, 0, 3), (3, 0, 1), (1, 1, 3))[i]
-        rows = pl.ds(part * (WIDE // 2), WIDE // 2)
-        source = across(offset)
-        target = across(4 - way + offset) if arriving else source
-        return remote(
-            buffer.at[source, rows], buffer.at[target, rows], sems.at[0, i], sems.at[1, i], tag=tag, sec=across(way)
-        )
-
-    def gather_sec(buffer, sems, tag, weights, total):
-        def came(i):
-            ring_copy(buffer, sems, tag, i, True).wait_recv()
-
-        total[...] = mm(weights[sec], buffer[sec])
-        came(0)
-        ring_copy(buffer, sems, tag, 4).start()
-        came(2)
-        ring_copy(buffer, sems, tag, 5).start()
-        came(1)
-        total[...] += mm(weights[across(3)], buffer[across(3)])
-        came(3)
-        total[...] += mm(weights[across(1)], buffer[across(1)])
-        came(4)
-        came(5)
-        total[...] += mm(weights[across(2)], buffer[across(2)])
-
-    def left(buffer, sems, tag):
-        for i in range(6):
-            ring_copy(buffer, sems, tag, i).wait_send()
-
-    for i in (0, 2, 1, 3):
-        ring_copy(feats, feat_sem, "feats", i).start()
+    widen(1 - half)
+    pool(1 - half, False, 0, SLOTS // 2)
+    ring_copy(feats, feat_sem, "feats", 0).start()
+    ring_copy(feats, feat_sem, "feats", 3).start()
+    pool(1 - half, False, SLOTS // 2, SLOTS)
+    ring_copy(feats, feat_sem, "feats", 2).start()
+    ring_copy(feats, feat_sem, "feats", 1).start()
     gather_sec(feats, feat_sem, "feats", expert_t, pre_e)
     hiddens[sec] = jax.nn.silu(pre_e[...]).astype(bf16)
     for i in (0, 2, 1, 3):
@@ -340,16 +343,10 @@
 
         core_copy(n).start()
 
-    def x_copy(n, d):
-        to = lax.rem(x + d, XS)
+    def x_copy(n, i):
+        to = lax.rem(x + (1, 3, 1, 3, 1, 3)[i], XS)
         return remote(
-            x_out.at[n, to], x_in.at[n, x], x_sem.at[n, 0, d], x_sem.at[n, 1, x], tag="x", emb=(to * ZS + z) * 2 + core
-        )
-
-    def x_arrive(n, d):
-        to = lax.rem(x + d, XS)
-        return remote(
-            x_out.at[n, to], x_in.at[n, to], x_sem.at[n, 0, d], x_sem.at[n, 1, to], tag="x", emb=(to * ZS + z) * 2 + core
+            x_out.at[n, i], x_in.at[n, i], x_sem.at[n, 0, i], x_sem.at[n, 1, i], tag="x", emb=(to * ZS + z) * 2 + core
         )
 
     def z_copy(n, d):
@@ -371,23 +368,40 @@
         def _(j):
             value = whole[n, 2 * j + core] + core_in[n, j].astype(f32)
             whole[n, 2 * j + core] = value
-            x_out[n, lax.div(j, ZS), lax.rem(j, ZS)] = value.astype(bf16)
-
-        for d in (2, 1, 3):
-            x_copy(n, d).start()
+
+        for i, (d, part) in enumerate(((2, 0), (2, 1), (1, 1), (3, 0))):
+
+            @pl.loop(0, ZS // 2)
+            def _(j):
+                x_out[n, i, j] = whole[n, place_of(d, part * (ZS // 2) + j)].astype(bf16)
+
+            x_copy(n, i).start()
+
+    def place_of(d, j):
+        return 2 * (lax.rem(x + d, XS) * ZS + j) + core
+
+    def x_relay(n):
+        for i, d in ((0, 1), (1, 3)):
+            x_copy(n, i).wait_recv()
+
+            @pl.loop(0, ZS // 2)
+            def _(j):
+                value = whole[n, place_of(d, i * (ZS // 2) + j)] + x_in[n, i, j].astype(f32)
+                x_out[n, 4 + i, j] = value.astype(bf16)
+
+            x_copy(n, 4 + i).start()
 
     def x_sum(n):
-        for d in (1, 3, 2):
-            x_arrive(n, d).wait_recv()
-
-        @pl.loop(0, ZS)
-        def _(j):
-            at = 2 * (x * ZS + j) + core
-            value = whole[n, at]
-            for d in range(1, XS):
-                value = value + x_in[n, lax.rem(x + d, XS), j].astype(f32)
-            whole[n, at] = value
-            z_out[n, j] = value.astype(bf16)
+        for part, (one, two) in enumerate(((3, 4), (2, 5))):
+            x_copy(n, one).wait_recv()
+            x_copy(n, two).wait_recv()
+
+            @pl.loop(0, ZS // 2)
+            def _(j):
+                at = part * (ZS // 2) + j
+                value = whole[n, place_of(0, at)] + x_in[n, one, j].astype(f32) + x_in[n, two, j].astype(f32)
+                whole[n, place_of(0, at)] = value
+                z_out[n, at] = value.astype(bf16)
 
         for d in range(1, ZS):
             z_copy(n, d).start()
@@ -399,8 +413,8 @@
         for d in range(1, ZS):
             value = value + z_in[n, lax.rem(z + d, ZS)].astype(f32)
         packed_ref[pl.ds(32 * n, 32), :] = value
-        for d in range(1, XS):
-            x_copy(n, d).wait_send()
+        for i in range(6):
+            x_copy(n, i).wait_send()
         for d in range(1, ZS):
             z_copy(n, d).wait_send()
 
@@ -439,8 +453,8 @@
     part_sum(0)
     expert_delta = (own_part[...] * silu_slope(pre_e[...])).astype(bf16)
     part(1, expert_ref, expert_delta)
+    x_relay(0)
     weight_grad(1, feats, expert_delta)
-    x_sum(0)
     core_sum(1)
     part_sum(1)
 
@@ -475,6 +489,11 @@
                 def _():
                     in_grads[me] = total[g * DIM : (g + 1) * DIM, h * CAP : (h + 1) * CAP]
 
+        @pl.when(t == 0)
+        def _():
+            x_relay(1)
+            x_sum(0)
+
     x_sum(1)
     z_sum(0)
     for d in range(1, ZS):
@@ -485,6 +504,13 @@
     packed_ref[64:72, :] = jnp.broadcast_to(head, (8, WIDE))
 
     grad_ref[...] = jnp.zeros((WIDE, ROWS), f32)
+
+    @pl.loop(1, EMB)
+    def _(d):
+        peer = lax.rem(me + d, EMB)
+        id_copy(peer, me).wait_send()
+        row_copy(peer, me).wait_send()
+
 
     @pl.loop(0, XS)
     def _(t):
@@ -522,9 +548,20 @@
     @pl.loop(1, EMB)
     def _(d):
         peer = lax.rem(me + d, EMB)
-        id_copy(peer, me).wait_send()
-        row_copy(peer, me).wait_send()
         grad_copy(peer, me).wait_send()
+
+
+def update_kernel(table_ref, accum_ref, grad_ref, packed_ref, new_table, new_accum, tower_grad, expert_grad, head_grad):
+    grad = grad_ref[...]
+    accum = accum_ref[...] + grad * grad
+    new_accum[...] = accum
+    new_table[...] = table_ref[...] - learn_rate * grad / jnp.sqrt(accum)
+
+    @pl.when(pl.program_id(0) == 0)
+    def _():
+        tower_grad[...] = packed_ref[:32, :]
+        expert_grad[...] = packed_ref[32:64, :]
+        head_grad[...] = packed_ref[64:65, :]
 
 
 def body(
@@ -577,8 +614,8 @@
             pltpu.VMEM((WIDE, BATCH), f32),
             pltpu.VMEM((2, 32, 32, WIDE), bf16),
             pltpu.VMEM((2, 32, 32, WIDE), bf16),
-            pltpu.VMEM((2, XS, ZS, 32, WIDE), bf16),
-            pltpu.VMEM((2, XS, ZS, 32, WIDE), bf16),
+            pltpu.VMEM((2, 6, ZS // 2, 32, WIDE), bf16),
+            pltpu.VMEM((2, 6, ZS // 2, 32, WIDE), bf16),
             pltpu.VMEM((2, ZS, 32, WIDE), bf16),
             pltpu.VMEM((2, ZS, 32, WIDE), bf16),
             pltpu.VMEM((2, 1, WIDE), f32),
@@ -599,7 +636,7 @@
             dma((2, SEC)),
             dma((2, 2, 6)),
             dma((2, 2)),
-            dma((2, 2, XS)),
+            dma((2, 2, 6)),
             dma((2, 2, ZS)),
             dma((2,)),
             dma((2, XS)),
@@ -619,9 +656,23 @@
         click_like.T,
         watch.reshape(1, BATCH),
     )
-    tower_grad, expert_grad, head_grad = packed[:32], packed[32:64], packed[64:65]
-    new_accum = accum + row_grad * row_grad
-    new_table = table - learn_rate * row_grad / jnp.sqrt(new_accum)
+    tile = pl.BlockSpec((128, ROWS), lambda i: (i, 0))
+    piece = pl.BlockSpec((32, WIDE), lambda i: (0, 0))
+    line = pl.BlockSpec((1, WIDE), lambda i: (0, 0))
+    whole_table = jax.ShapeDtypeStruct((SLOTS * DIM, ROWS), f32)
+    new_table, new_accum, tower_grad, expert_grad, head_grad = pl.pallas_call(
+        update_kernel,
+        grid=(SLOTS * DIM // 128,),
+        out_shape=(
+            whole_table,
+            whole_table,
+            jax.ShapeDtypeStruct((32, WIDE), f32),
+            jax.ShapeDtypeStruct((32, WIDE), f32),
+            jax.ShapeDtypeStruct((1, WIDE), f32),
+        ),
+        in_specs=[tile, tile, tile, pl.BlockSpec((72, WIDE), lambda i: (0, 0))],
+        out_specs=(tile, tile, piece, piece, line),
+    )(table, accum, row_grad, packed)
 
     def back(value):
         return value.reshape(SLOTS, DIM, ROWS).transpose(0, 2, 1)

time: 149 us -> 147 us (0.987)
  Pallas kernels: 142 us -> 145 us
  other arithmetic: 2.85 us -> 0 us
  local copies, waits for them, and re-layouts: 2.83 us -> 0 us
    pallas_call x0 -> x1, Pallas kernels: none -> 4.36 us  [body(): pl.pallas_call(update_kernel, grid=(SLOTS * DIM // 128,), out_shape=(whol...]
    sub x1 -> x0, other arithmetic: 2.85 us -> none  [body(): new_table = table - learn_rate * row_grad / jnp.sqrt(new_accum)]
    slice x2 -> x0, local copies, waits for them, and re-layouts: 2.82 us -> none  [the longest x1 1.53 us: body(): packed[:32]]
where the time goes in v4:
time: 147 us
  Pallas kernels  145 us (99%)
    pallas_call x1, Pallas kernels, body(): pl.pallas_call(step_kernel, out_shape=(jax.ShapeDtypeStruct((SLOTS * DIM,...  141 us
    pallas_call x1, Pallas kernels, body(): pl.pallas_call(update_kernel, grid=(SLOTS * DIM // 128,), out_shape=(whol...  4.36 us

profile of v4, /device:TPU:1, one launch (start us, length us, event | category | flops | bytes accessed | tf_op | source)
XLA Modules:
  0.0 146.5 jit_solution(10943987449791997161)
XLA Ops:
  1.3 140.9 %shard_map.137 = (f32[512,512]{1,0:T(8,128)}, f32[72,512]{1,0:T(8,128)}) custom-call(s32[1]{0:T(128)S(6)} %copy.15.task_ref, s32[8,2,256]{2,1,0:T(2,128)} %bitcast.19, s32[8,256]{1,0:T(8,128)} %bitcast.20, f32[512,512]{1,0:T(8,128)} %bitcast.16, bf16[2048,512]{1,0:T(8,128)(2,1)} %expert_hbm.1, bf16[2048,512]{1,0:T(8,128)(2,1)} %tower_hbm.1, ...), custom_call_target="tpu_custom_call" | custom-call | tf_op jit(solution)/shard_map/pallas_call | solution.py:584
  142.2 4.4 %shard_map.138 = (f32[512,512]{1,0:T(8,128)}, f32[512,512]{1,0:T(8,128)}, f32[32,512]{1,0:T(8,128)}, f32[32,512]{1,0:T(8,128)}, f32[1,512]{1,0:T(1,128)}) custom-call(f32[512,512]{1,0:T(8,128)} %bitcast.17, f32[512,512]{1,0:T(8,128)} %bitcast.18, f32[512,512]{1,0:T(8,128)} %get-tuple-element.12.grad_ref, f32[72,512]{1,0:T(8,128)} %get-tuple-element.13.packed_ref), custom_call_target="tpu_custom_call" | custom-call | tf_op jit(solution)/shard_map/pallas_call | solution.py:663

commit v5 on v4

--- a/solution.py
+++ b/solution.py
@@ -134,9 +134,14 @@
         group = lax.rem(half + lax.div(d, 32), 2)
         return group * 32 + lax.rem(inner + d, 32)
 
-    def behind(d):
-        group = lax.rem(half + lax.div(d, 32), 2)
-        return group * 32 + lax.rem(inner + 64 - d, 32)
+    def z_shift(i):
+        step, odd = lax.div(i + 1, 2), lax.rem(i, 2)
+        return lax.rem(step * odd + (ZS - step) * (1 - odd), ZS)
+
+    def chip(t, way):
+        group = lax.rem(half + lax.div(t, 16), 2)
+        column = 2 * group + lax.rem(x + lax.div(t, ZS), 2)
+        return (column * ZS + lax.rem(z + ZS + way * z_shift(lax.rem(t, ZS)), ZS)) * 2
 
     def id_copy(peer, at):
         return remote(ob.at[peer], ib.at[at], id_send.at[peer], id_recv.at[at], tag="ids", emb=peer)
@@ -183,9 +188,15 @@
         for i in range(6):
             ring_copy(buffer, sems, tag, i).wait_send()
 
-    @pl.loop(1, EMB)
-    def _(d):
-        id_copy(ahead(d), me).start()
+    @pl.loop(0, EMB // 2)
+    def _(t):
+        base = chip(t, 1)
+
+        @pl.when(t > 0)
+        def _():
+            id_copy(base + core, me).start()
+
+        id_copy(base + 1 - core, me).start()
 
     ib[me] = ob[me]
     tb[...] = table_ref[...].astype(bf16)
@@ -201,8 +212,8 @@
 
     @pl.loop(0, EMB // 2)
     def _(t):
-        a = behind(2 * t)
-        b = behind(2 * t + 1)
+        a = chip(t, -1) + core
+        b = chip(t, -1) + 1 - core
 
         @pl.when(t > 0)
         def _():
@@ -435,11 +446,15 @@
     )
     hc_copy().start()
     weight_grad(0, hiddens, tower_delta)
+    part_sum(0)
+    expert_delta = (own_part[...] * silu_slope(pre_e[...])).astype(bf16)
+    part(1, expert_ref, expert_delta)
+    core_sum(0)
     hc_copy().wait()
     head_x[x] = head_core[0] + head_core[1]
     for d in range(1, XS):
         hx_copy(d, x).start()
-    core_sum(0)
+    weight_grad(1, feats, expert_delta)
     left(feats, feat_sem, "feats")
     left(hiddens, hidden_sem, "hiddens")
     for d in (2, 1, 3):
@@ -449,13 +464,6 @@
     head_z[z] = (head_x[0] + head_x[1]) + (head_x[2] + head_x[3])
     for d in range(1, ZS):
         hz_copy(d, z).start()
-
-    part_sum(0)
-    expert_delta = (own_part[...] * silu_slope(pre_e[...])).astype(bf16)
-    part(1, expert_ref, expert_delta)
-    x_relay(0)
-    weight_grad(1, feats, expert_delta)
-    core_sum(1)
     part_sum(1)
 
     @pl.loop(0, SLOTS)
@@ -481,18 +489,29 @@
                 peer = (2 * pair + h) * 8 + g
                 out_grads[peer] = total[g * DIM : (g + 1) * DIM, h * CAP : (h + 1) * CAP]
 
+        @pl.when(t == 0)
+        def _():
+            in_grads[me] = out_grads[me]
+
+        @pl.loop(0, ZS)
+        def _(j):
+            base = (pair * ZS + lax.rem(z + z_shift(j), ZS)) * 2
+            for c in range(2):
+                peer = base + c
+
                 @pl.when(peer != me)
                 def _():
                     grad_copy(peer, me).start()
 
-                @pl.when(peer == me)
-                def _():
-                    in_grads[me] = total[g * DIM : (g + 1) * DIM, h * CAP : (h + 1) * CAP]
-
         @pl.when(t == 0)
         def _():
+            core_sum(1)
+            x_relay(0)
+
+        @pl.when(t == 1)
+        def _():
+            x_sum(0)
             x_relay(1)
-            x_sum(0)
 
     x_sum(1)
     z_sum(0)

time: 147 us -> 145 us (0.986)
  Pallas kernels: 145 us -> 142 us
    pallas_call x1, Pallas kernels: 141 us -> 137 us  [body(): pl.pallas_call(step_kernel, out_shape=(jax.ShapeDtypeStruct((SLOTS * DIM,...]
where the time goes in v5:
time: 145 us; the launch traced here: 143 us
  Pallas kernels  142 us (98%)
    pallas_call x1, Pallas kernels, body(): pl.pallas_call(step_kernel, out_shape=(jax.ShapeDtypeStruct((SLOTS * DIM,...  137 us
    pallas_call x1, Pallas kernels, body(): pl.pallas_call(update_kernel, grid=(SLOTS * DIM // 128,), out_shape=(whol...  4.36 us

profile of v5, /device:TPU:1, one launch (start us, length us, event | category | flops | bytes accessed | tf_op | source)
XLA Modules:
  0.0 143.1 jit_solution(9712140843385827819)
XLA Ops:
  1.3 137.5 %shard_map.137 = (f32[512,512]{1,0:T(8,128)}, f32[72,512]{1,0:T(8,128)}) custom-call(s32[1]{0:T(128)S(6)} %copy.15.task_ref, s32[8,2,256]{2,1,0:T(2,128)} %bitcast.19, s32[8,256]{1,0:T(8,128)} %bitcast.20, f32[512,512]{1,0:T(8,128)} %bitcast.16, bf16[2048,512]{1,0:T(8,128)(2,1)} %expert_hbm.1, bf16[2048,512]{1,0:T(8,128)(2,1)} %tower_hbm.1, ...), custom_call_target="tpu_custom_call" | custom-call | tf_op jit(solution)/shard_map/pallas_call | solution.py:603
  138.7 4.4 %shard_map.138 = (f32[512,512]{1,0:T(8,128)}, f32[512,512]{1,0:T(8,128)}, f32[32,512]{1,0:T(8,128)}, f32[32,512]{1,0:T(8,128)}, f32[1,512]{1,0:T(1,128)}) custom-call(f32[512,512]{1,0:T(8,128)} %bitcast.17, f32[512,512]{1,0:T(8,128)} %bitcast.18, f32[512,512]{1,0:T(8,128)} %get-tuple-element.12.grad_ref, f32[72,512]{1,0:T(8,128)} %get-tuple-element.13.packed_ref), custom_call_target="tpu_custom_call" | custom-call | tf_op jit(solution)/shard_map/pallas_call | solution.py:682

commit v6 on v5

--- a/solution.py
+++ b/solution.py
@@ -446,24 +446,25 @@
     )
     hc_copy().start()
     weight_grad(0, hiddens, tower_delta)
-    part_sum(0)
-    expert_delta = (own_part[...] * silu_slope(pre_e[...])).astype(bf16)
-    part(1, expert_ref, expert_delta)
-    core_sum(0)
     hc_copy().wait()
     head_x[x] = head_core[0] + head_core[1]
     for d in range(1, XS):
         hx_copy(d, x).start()
-    weight_grad(1, feats, expert_delta)
-    left(feats, feat_sem, "feats")
-    left(hiddens, hidden_sem, "hiddens")
-    for d in (2, 1, 3):
-        sec_copy(shares, share_sem, "shares", d, sec).wait_send()
+    part_sum(0)
+    expert_delta = (own_part[...] * silu_slope(pre_e[...])).astype(bf16)
+    part(1, expert_ref, expert_delta)
     for d in range(1, XS):
         hx_copy(d, lax.rem(x + d, XS)).wait_recv()
     head_z[z] = (head_x[0] + head_x[1]) + (head_x[2] + head_x[3])
     for d in range(1, ZS):
         hz_copy(d, z).start()
+    core_sum(0)
+    weight_grad(1, feats, expert_delta)
+    x_relay(0)
+    left(feats, feat_sem, "feats")
+    left(hiddens, hidden_sem, "hiddens")
+    for d in (2, 1, 3):
+        sec_copy(shares, share_sem, "shares", d, sec).wait_send()
     part_sum(1)
 
     @pl.loop(0, SLOTS)
@@ -506,11 +507,10 @@
         @pl.when(t == 0)
         def _():
             core_sum(1)
-            x_relay(0)
+            x_sum(0)
 
         @pl.when(t == 1)
         def _():
-            x_sum(0)
             x_relay(1)
 
     x_sum(1)
@@ -571,16 +571,17 @@
 
 
 def update_kernel(table_ref, accum_ref, grad_ref, packed_ref, new_table, new_accum, tower_grad, expert_grad, head_grad):
-    grad = grad_ref[...]
-    accum = accum_ref[...] + grad * grad
-    new_accum[...] = accum
-    new_table[...] = table_ref[...] - learn_rate * grad / jnp.sqrt(accum)
-
-    @pl.when(pl.program_id(0) == 0)
-    def _():
-        tower_grad[...] = packed_ref[:32, :]
-        expert_grad[...] = packed_ref[32:64, :]
-        head_grad[...] = packed_ref[64:65, :]
+    @pl.loop(0, SLOTS)
+    def _(s):
+        rows = pl.ds(pl.multiple_of(s * DIM, DIM), DIM)
+        grad = grad_ref[rows, :]
+        accum = accum_ref[rows, :] + grad * grad
+        new_accum[rows, :] = accum
+        new_table[rows, :] = table_ref[rows, :] - learn_rate * grad / jnp.sqrt(accum)
+
+    tower_grad[...] = packed_ref[:32, :]
+    expert_grad[...] = packed_ref[32:64, :]
+    head_grad[...] = packed_ref[64:65, :]
 
 
 def body(
@@ -663,7 +664,7 @@
             dma((EMB,)),
             dma((EMB,)),
         ],
-        compiler_params=pltpu.CompilerParams(collective_id=0, has_side_effects=True, vmem_limit_bytes=60 << 20),
+        compiler_params=pltpu.CompilerParams(collective_id=0, has_side_effects=True, vmem_limit_bytes=52 << 20),
     )(
         section_task,
         slot_ids.transpose(1, 2, 0),
@@ -675,13 +676,9 @@
         click_like.T,
         watch.reshape(1, BATCH),
     )
-    tile = pl.BlockSpec((128, ROWS), lambda i: (i, 0))
-    piece = pl.BlockSpec((32, WIDE), lambda i: (0, 0))
-    line = pl.BlockSpec((1, WIDE), lambda i: (0, 0))
     whole_table = jax.ShapeDtypeStruct((SLOTS * DIM, ROWS), f32)
     new_table, new_accum, tower_grad, expert_grad, head_grad = pl.pallas_call(
         update_kernel,
-        grid=(SLOTS * DIM // 128,),
         out_shape=(
             whole_table,
             whole_table,
@@ -689,8 +686,9 @@
             jax.ShapeDtypeStruct((32, WIDE), f32),
             jax.ShapeDtypeStruct((1, WIDE), f32),
         ),
-        in_specs=[tile, tile, tile, pl.BlockSpec((72, WIDE), lambda i: (0, 0))],
-        out_specs=(tile, tile, piece, piece, line),
+        in_specs=[vmem] * 4,
+        out_specs=(vmem,) * 5,
+        compiler_params=pltpu.CompilerParams(vmem_limit_bytes=16 << 20),
     )(table, accum, row_grad, packed)
 
     def back(value):

time: 145 us -> 140 us (0.966); the launches traced: 143 us -> 140 us
  Pallas kernels: 142 us -> 135 us
  local copies, waits for them, and re-layouts: 0 us -> 3.45 us
    pallas_call x1, Pallas kernels: 137 us -> 134 us  [body(): pl.pallas_call(step_kernel, out_shape=(jax.ShapeDtypeStruct((SLOTS * DIM,...]
    unnamed x0 -> x14, local copies, waits for them, and re-layouts: none -> 3.45 us
    pallas_call x1, Pallas kernels: 4.36 us -> 1.88 us  [body(): pl.pallas_call(update_kernel, out_shape=(whole_table, whole_table, jax.Sh...]
where the time goes in v6:
time: 140 us
  Pallas kernels  135 us (96%)
  local copies, waits for them, and re-layouts  3.45 us (2%)
    pallas_call x1, Pallas kernels, body(): pl.pallas_call(step_kernel, out_shape=(jax.ShapeDtypeStruct((SLOTS * DIM,...  134 us
    unnamed x14, local copies, waits for them, and re-layouts  3.45 us

profile of v6, /device:TPU:1, one launch (start us, length us, event | category | flops | bytes accessed | tf_op | source)
XLA Modules:
  0.0 140.2 jit_solution(15675087960842781676)
XLA Ops:
  1.3 0.0 copy-start.2
  1.3 0.7 copy-done.2
  2.0 0.0 copy-start.3
  2.0 0.7 copy-done.3
  2.7 0.0 copy-start.4
  2.7 0.7 copy-done.4
  3.4 0.0 copy-start.5
  3.4 0.7 copy-done.5
  4.1 0.0 copy-start.6
  4.1 0.7 copy-done.6
  4.7 0.0 copy-start
  4.7 0.0 copy-start.1
  4.7 133.5 %shard_map.137 = (f32[512,512]{1,0:T(8,128)S(1)}, f32[72,512]{1,0:T(8,128)S(1)}) custom-call(s32[1]{0:T(128)S(6)} %copy.15.task_ref, s32[8,2,256]{2,1,0:T(2,128)S(1)} %bitcast.19, s32[8,256]{1,0:T(8,128)S(1)} %bitcast.20, f32[512,512]{1,0:T(8,128)} %bitcast.16, bf16[2048,512]{1,0:T(8,128)(2,1)} %expert_hbm.1, bf16[2048,512]{1,0:T(8,128)(2,1)} %tower_hbm.1, ...), custom_call_target="tpu_custom_call" | custom-call | tf_op jit(solution)/shard_map/pallas_call | solution.py:604
  138.3 0.0 copy-done
  138.3 0.0 copy-done.1
  138.3 1.9 %shard_map.138 = (f32[512,512]{1,0:T(8,128)}, f32[512,512]{1,0:T(8,128)}, f32[32,512]{1,0:T(8,128)}, f32[32,512]{1,0:T(8,128)}, f32[1,512]{1,0:T(1,128)}) custom-call(f32[512,512]{1,0:T(8,128)S(1)} %bitcast.17, f32[512,512]{1,0:T(8,128)S(1)} %bitcast.18, f32[512,512]{1,0:T(8,128)S(1)} %get-tuple-element.12.grad_ref, f32[72,512]{1,0:T(8,128)S(1)} %get-tuple-element.13.packed_ref), custom_call_target="tpu_custom_call" | custom-call | tf_op jit(solution)/shard_map/pallas_call | solution.py:680
Async XLA Ops:
  1.3 0.7 copy-start.2
  2.0 0.7 copy-start.3
  2.7 0.7 copy-start.4
  3.4 0.7 copy-start.5
  4.1 0.7 copy-start.6
  4.7 133.6 %copy-start = (f32[8,512,64]{1,2,0:T(8,128)S(1)}, f32[8,512,64]{1,2,0:T(8,128)}, u32[]{:S(2)}) copy-start(f32[8,512,64]{1,2,0:T(8,128)} %param.10) | copy-start | bytes 3145732
  4.7 133.6 %copy-start.1 = (f32[8,512,64]{1,2,0:T(8,128)S(1)}, f32[8,512,64]{1,2,0:T(8,128)}, u32[]{:S(2)}) copy-start(f32[8,512,64]{1,2,0:T(8,128)} %param.11) | copy-start | bytes 3145732

commit v7 on v6

--- a/solution.py
+++ b/solution.py
@@ -241,11 +241,11 @@
 
         row_copy(b, me).start()
 
-    def widen(part):
-        for h in range(4):
-            wide_rows[:, h * CAP : (h + 1) * CAP] = in_rows[pl.ds((part * 4 + h) * 8, 8)].reshape(8 * DIM, CAP)
-
-    def pool(part, first, begin, end):
+    def widen(base, slabs):
+        for h in range(slabs):
+            wide_rows[:, h * CAP : (h + 1) * CAP] = in_rows[pl.ds((base + h) * 8, 8)].reshape(8 * DIM, CAP)
+
+    def pool(base, slabs, first, last, begin, end):
         @pl.loop(begin, end)
         def _(s):
             rows = pl.ds(pl.multiple_of(s * DIM, DIM), DIM)
@@ -254,33 +254,40 @@
                 place = pos[2 * s + k]
                 shard = place >> 7
                 low = jnp.where(bag_ref[pl.ds(s, 1), :] > k, shard & 7, -1)
-                key = ((shard >> 3) - part * 4) * CAP + (place & (CAP - 1))
-                picked = mm(wide_rows[...], hot(4 * CAP, key))
+                key = ((shard >> 3) - base) * CAP + (place & (CAP - 1))
+                picked = mm(wide_rows[:, : slabs * CAP], hot(slabs * CAP, key))
                 for g in range(8):
                     pooled = pooled + jnp.where(low == g, picked[g * DIM : (g + 1) * DIM], 0.0)
-            if first:
+            if last:
+                feats[sec, rows, :] = pooled.astype(bf16)
+            else:
                 pooled_ref[rows, :] = pooled
-            else:
-                feats[sec, rows, :] = pooled.astype(bf16)
 
     @pl.loop(1, 32)
     def _(d):
         peer = ahead(d)
         row_copy(peer, peer).wait_recv()
 
-    widen(half)
-    pool(half, True, 0, SLOTS)
-
-    @pl.loop(32, EMB)
-    def _(d):
-        peer = ahead(d)
-        row_copy(peer, peer).wait_recv()
-
-    widen(1 - half)
-    pool(1 - half, False, 0, SLOTS // 2)
+    widen(4 * half, 4)
+    pool(4 * half, 4, True, False, 0, SLOTS)
+
+    def column_came(column):
+        @pl.loop(0, 16)
+        def _(j):
+            peer = column * 16 + j
+            row_copy(peer, peer).wait_recv()
+
+    near = 2 * (1 - half) + lax.rem(x, 2)
+    far = 2 * (1 - half) + lax.rem(x + 1, 2)
+    column_came(near)
+    widen(2 * near, 2)
+    pool(2 * near, 2, False, False, 0, SLOTS)
+    column_came(far)
+    widen(2 * far, 2)
+    pool(2 * far, 2, False, True, 0, SLOTS // 2)
     ring_copy(feats, feat_sem, "feats", 0).start()
     ring_copy(feats, feat_sem, "feats", 3).start()
-    pool(1 - half, False, SLOTS // 2, SLOTS)
+    pool(2 * far, 2, False, True, SLOTS // 2, SLOTS)
     ring_copy(feats, feat_sem, "feats", 2).start()
     ring_copy(feats, feat_sem, "feats", 1).start()
     gather_sec(feats, feat_sem, "feats", expert_t, pre_e)
@@ -461,6 +468,7 @@
     core_sum(0)
     weight_grad(1, feats, expert_delta)
     x_relay(0)
+    core_sum(1)
     left(feats, feat_sem, "feats")
     left(hiddens, hidden_sem, "hiddens")
     for d in (2, 1, 3):
@@ -506,12 +514,8 @@
 
         @pl.when(t == 0)
         def _():
-            core_sum(1)
+            x_relay(1)
             x_sum(0)
-
-        @pl.when(t == 1)
-        def _():
-            x_relay(1)
 
     x_sum(1)
     z_sum(0)

time: 140 us -> 143 us (1.021)
  Pallas kernels: 135 us -> 138 us
    pallas_call x1, Pallas kernels: 134 us -> 136 us  [body(): pl.pallas_call(step_kernel, out_shape=(jax.ShapeDtypeStruct((SLOTS * DIM,...]
where the time goes in v7:
time: 143 us
  Pallas kernels  138 us (97%)
  local copies, waits for them, and re-layouts  3.45 us (2%)
    pallas_call x1, Pallas kernels, body(): pl.pallas_call(step_kernel, out_shape=(jax.ShapeDtypeStruct((SLOTS * DIM,...  136 us
    unnamed x14, local copies, waits for them, and re-layouts  3.45 us

profile of v7, /device:TPU:1, one launch (start us, length us, event | category | flops | bytes accessed | tf_op | source)
XLA Modules:
  0.0 142.8 jit_solution(17185530377109710536)
XLA Ops:
  1.3 0.0 copy-start.2
  1.3 0.7 copy-done.2
  2.0 0.0 copy-start.3
  2.0 0.7 copy-done.3
  2.7 0.0 copy-start.4
  2.7 0.7 copy-done.4
  3.4 0.0 copy-start.5
  3.4 0.7 copy-done.5
  4.1 0.0 copy-start.6
  4.1 0.7 copy-done.6
  4.7 0.0 copy-start
  4.7 0.0 copy-start.1
  4.7 136.2 %shard_map.137 = (f32[512,512]{1,0:T(8,128)S(1)}, f32[72,512]{1,0:T(8,128)S(1)}) custom-call(s32[1]{0:T(128)S(6)} %copy.15.task_ref, s32[8,2,256]{2,1,0:T(2,128)S(1)} %bitcast.19, s32[8,256]{1,0:T(8,128)S(1)} %bitcast.20, f32[512,512]{1,0:T(8,128)} %bitcast.16, bf16[2048,512]{1,0:T(8,128)(2,1)} %expert_hbm.1, bf16[2048,512]{1,0:T(8,128)(2,1)} %tower_hbm.1, ...), custom_call_target="tpu_custom_call" | custom-call | tf_op jit(solution)/shard_map/pallas_call | solution.py:608
  140.9 0.0 copy-done
  140.9 0.0 copy-done.1
  140.9 1.9 %shard_map.138 = (f32[512,512]{1,0:T(8,128)}, f32[512,512]{1,0:T(8,128)}, f32[32,512]{1,0:T(8,128)}, f32[32,512]{1,0:T(8,128)}, f32[1,512]{1,0:T(1,128)}) custom-call(f32[512,512]{1,0:T(8,128)S(1)} %bitcast.17, f32[512,512]{1,0:T(8,128)S(1)} %bitcast.18, f32[512,512]{1,0:T(8,128)S(1)} %get-tuple-element.12.grad_ref, f32[72,512]{1,0:T(8,128)S(1)} %get-tuple-element.13.packed_ref), custom_call_target="tpu_custom_call" | custom-call | tf_op jit(solution)/shard_map/pallas_call | solution.py:684
Async XLA Ops:
  1.3 0.7 copy-start.2
  2.0 0.7 copy-start.3
  2.7 0.7 copy-start.4
  3.4 0.7 copy-start.5
  4.1 0.7 copy-start.6
  4.7 136.2 %copy-start = (f32[8,512,64]{1,2,0:T(8,128)S(1)}, f32[8,512,64]{1,2,0:T(8,128)}, u32[]{:S(2)}) copy-start(f32[8,512,64]{1,2,0:T(8,128)} %param.10) | copy-start | bytes 3145732
  4.7 136.2 %copy-start.1 = (f32[8,512,64]{1,2,0:T(8,128)S(1)}, f32[8,512,64]{1,2,0:T(8,128)}, u32[]{:S(2)}) copy-start(f32[8,512,64]{1,2,0:T(8,128)} %param.11) | copy-start | bytes 3145732

commit v8 on v7

--- a/solution.py
+++ b/solution.py
@@ -468,7 +468,6 @@
     core_sum(0)
     weight_grad(1, feats, expert_delta)
     x_relay(0)
-    core_sum(1)
     left(feats, feat_sem, "feats")
     left(hiddens, hidden_sem, "hiddens")
     for d in (2, 1, 3):
@@ -514,8 +513,12 @@
 
         @pl.when(t == 0)
         def _():
+            core_sum(1)
+            x_sum(0)
+
+        @pl.when(t == 1)
+        def _():
             x_relay(1)
-            x_sum(0)
 
     x_sum(1)
     z_sum(0)

time: 143 us -> 140 us (0.979)
  Pallas kernels: 138 us -> 135 us
    pallas_call x1, Pallas kernels: 136 us -> 133 us  [body(): pl.pallas_call(step_kernel, out_shape=(jax.ShapeDtypeStruct((SLOTS * DIM,...]
where the time goes in v8:
time: 140 us; the launch traced here: 139 us
  Pallas kernels  135 us (96%)
  local copies, waits for them, and re-layouts  3.45 us (2%)
    pallas_call x1, Pallas kernels, body(): pl.pallas_call(step_kernel, out_shape=(jax.ShapeDtypeStruct((SLOTS * DIM,...  133 us
    unnamed x14, local copies, waits for them, and re-layouts  3.45 us

profile of v8, /device:TPU:1, one launch (start us, length us, event | category | flops | bytes accessed | tf_op | source)
XLA Modules:
  0.0 139.3 jit_solution(4687042892604240976)
XLA Ops:
  1.3 0.0 copy-start.2
  1.3 0.7 copy-done.2
  2.0 0.0 copy-start.3
  2.0 0.7 copy-done.3
  2.7 0.0 copy-start.4
  2.7 0.7 copy-done.4
  3.4 0.0 copy-start.5
  3.4 0.7 copy-done.5
  4.1 0.0 copy-start.6
  4.1 0.7 copy-done.6
  4.7 0.0 copy-start
  4.7 0.0 copy-start.1
  4.7 132.7 %shard_map.137 = (f32[512,512]{1,0:T(8,128)S(1)}, f32[72,512]{1,0:T(8,128)S(1)}) custom-call(s32[1]{0:T(128)S(6)} %copy.15.task_ref, s32[8,2,256]{2,1,0:T(2,128)S(1)} %bitcast.19, s32[8,256]{1,0:T(8,128)S(1)} %bitcast.20, f32[512,512]{1,0:T(8,128)} %bitcast.16, bf16[2048,512]{1,0:T(8,128)(2,1)} %expert_hbm.1, bf16[2048,512]{1,0:T(8,128)(2,1)} %tower_hbm.1, ...), custom_call_target="tpu_custom_call" | custom-call | tf_op jit(solution)/shard_map/pallas_call | solution.py:611
  137.4 0.0 copy-done
  137.4 0.0 copy-done.1
  137.4 1.9 %shard_map.138 = (f32[512,512]{1,0:T(8,128)}, f32[512,512]{1,0:T(8,128)}, f32[32,512]{1,0:T(8,128)}, f32[32,512]{1,0:T(8,128)}, f32[1,512]{1,0:T(1,128)}) custom-call(f32[512,512]{1,0:T(8,128)S(1)} %bitcast.17, f32[512,512]{1,0:T(8,128)S(1)} %bitcast.18, f32[512,512]{1,0:T(8,128)S(1)} %get-tuple-element.12.grad_ref, f32[72,512]{1,0:T(8,128)S(1)} %get-tuple-element.13.packed_ref), custom_call_target="tpu_custom_call" | custom-call | tf_op jit(solution)/shard_map/pallas_call | solution.py:687
Async XLA Ops:
  1.3 0.7 copy-start.2
  2.0 0.7 copy-start.3
  2.7 0.7 copy-start.4
  3.4 0.7 copy-start.5
  4.1 0.7 copy-start.6
  4.7 132.7 %copy-start = (f32[8,512,64]{1,2,0:T(8,128)S(1)}, f32[8,512,64]{1,2,0:T(8,128)}, u32[]{:S(2)}) copy-start(f32[8,512,64]{1,2,0:T(8,128)} %param.10) | copy-start | bytes 3145732
  4.7 132.7 %copy-start.1 = (f32[8,512,64]{1,2,0:T(8,128)S(1)}, f32[8,512,64]{1,2,0:T(8,128)}, u32[]{:S(2)}) copy-start(f32[8,512,64]{1,2,0:T(8,128)} %param.11) | copy-start | bytes 3145732
